TPU v7x, 32 devices: a whole 2x2x4 slice. The times are simulated.
32 devices in a mesh: expert: 8 (over z, x), dp: 4 (over y, core).
Axes of the slice: x: 2, y: 2, z: 4, core: 2. Of those that a mesh axis runs over, the one named last changes fastest.
Arguments:
- tokens: bfloat16 [4096, 2048], P(('expert', 'dp')), may hold values from -6 to 6
- out_grad: bfloat16 [4096, 2048], P(('expert', 'dp')), may hold values from -6 to 6
- route_weights: bfloat16 [4096, 8], P(('expert', 'dp')), may hold values from 0.05 to 2.5, as said below
- expert_ids: int32 [4096, 8], P(('expert', 'dp')), may hold values from 0 to 15, all different within a row; in each aligned block of 128 rows (0 to 127, 128 to 255, ...) at most 96 rows name the same one
- gate_weight: bfloat16 [16, 2048, 384], P('expert'), may hold values from -0.125 to 0.125
- up_weight: bfloat16 [16, 2048, 384], P('expert'), may hold values from -0.125 to 0.125
- down_weight: bfloat16 [16, 384, 2048], P('expert'), may hold values from -0.3125 to 0.3125
Outputs:
- grad_input: bfloat16 [4096, 2048], P(('expert', 'dp'))
- grad_gate: bfloat16 [16, 2048, 384], P('expert', 'dp')
- grad_up: bfloat16 [16, 2048, 384], P('expert', 'dp')
- grad_down: bfloat16 [16, 384, 2048], P('expert', 'dp')
- expert_load: float32 [16], replicated
Inputs may be any that keep to these rules, and one draw needn't show every extreme that they name: `expert_ids`: each row names 8 different experts. Within each aligned block of 128 rows (the rows of one device) no expert is named by more than 96 rows, a bound that some block reaches. `route_weights`: positive router weights.
All inputs are finite; a program needn't handle non-finite values.
Results may differ from a plain program's by a relative error of at most 0.009.
Values may be sent and summed in bfloat16 or wider, within the bound.
No kernel may reach another device: no remote copies, remote signals or barrier semaphores. Data moves between devices by JAX's collectives and lax.ppermute only.
A program may use at most 192 MiB of HBM per device.

v0:
```python
import jax
import jax.numpy as jnp
from jax import lax
from jax.sharding import PartitionSpec as P


def swiglu_grads(token_rows, grad_rows, route_rows, gate_matrix, up_matrix, down_matrix):
    contract_last = (((1,), (1,)), ((), ()))
    contract_first = (((0,), (0,)), ((), ()))
    gate_linear = jnp.dot(token_rows, gate_matrix, preferred_element_type=jnp.float32)
    up_linear = jnp.dot(token_rows, up_matrix, preferred_element_type=jnp.float32)
    logistic = jax.nn.sigmoid(gate_linear)
    activated = gate_linear * logistic
    hidden = (activated * up_linear).astype(jnp.bfloat16)
    scaled = (route_rows.astype(jnp.float32)[:, None] * grad_rows.astype(jnp.float32)).astype(
        jnp.bfloat16
    )
    delta_hidden = lax.dot_general(
        scaled, down_matrix, contract_last, preferred_element_type=jnp.float32
    )
    delta_gate = (
        delta_hidden * up_linear * logistic * (1.0 + gate_linear * (1.0 - logistic))
    ).astype(jnp.bfloat16)
    delta_up = (delta_hidden * activated).astype(jnp.bfloat16)
    pair_grad = lax.dot_general(
        delta_gate, gate_matrix, contract_last, preferred_element_type=jnp.float32
    )
    pair_grad = pair_grad + lax.dot_general(
        delta_up, up_matrix, contract_last, preferred_element_type=jnp.float32
    )
    gate_part = lax.dot_general(
        token_rows, delta_gate, contract_first, preferred_element_type=jnp.float32
    )
    up_part = lax.dot_general(
        token_rows, delta_up, contract_first, preferred_element_type=jnp.float32
    )
    down_part = lax.dot_general(hidden, scaled, contract_first, preferred_element_type=jnp.float32)
    return (pair_grad, gate_part, up_part, down_part)


def padded_grads(token_rows, grad_rows, route_rows, gate_matrix, up_matrix, down_matrix):
    pair_grad, gate_part, up_part, down_part = swiglu_grads(
        token_rows, grad_rows, route_rows, gate_matrix, up_matrix, down_matrix
    )
    return (pair_grad.astype(jnp.bfloat16), gate_part, up_part, down_part)


def run_rows(token_rows, grad_rows, route_rows, gate_matrix, up_matrix, down_matrix):
    result = padded_grads(token_rows, grad_rows, route_rows, gate_matrix, up_matrix, down_matrix)
    rounded = lax.optimization_barrier(
        (
            result[1].astype(jnp.bfloat16),
            result[2].astype(jnp.bfloat16),
            result[3].astype(jnp.bfloat16),
        )
    )
    return (result[0], rounded[0], rounded[1], rounded[2])


def shards(tokens, out_grad, route_weights, expert_ids, gate_weight, up_weight, down_weight):
    local_experts = gate_weight.shape[0]
    axis_devices = lax.axis_size("expert")
    data_groups = lax.axis_size("dp")
    num_experts = local_experts * axis_devices
    local_tokens, top_count = expert_ids.shape
    model_width = tokens.shape[1]
    capacity = local_tokens * top_count * 3 // (2 * num_experts)
    half_axis = axis_devices // 2
    expert_iota = jnp.arange(num_experts, dtype=jnp.int32)
    chosen = expert_ids[:, :, None] == expert_iota
    per_token = jnp.sum(chosen.astype(jnp.int32), axis=1)
    local_count = jnp.sum(per_token, axis=0).astype(jnp.float32)
    local_weight = jnp.sum(
        jnp.where(chosen, route_weights.astype(jnp.float32)[:, :, None], 0.0), axis=(0, 1)
    )
    global_count, global_weight = lax.psum((local_count, local_weight), ("expert", "dp"))
    expert_load = global_weight * (
        num_experts / (local_tokens * axis_devices * data_groups * top_count)
    )
    earlier = jnp.cumsum(per_token, axis=0) - per_token
    rank_in_block = jnp.take_along_axis(earlier, expert_ids, axis=1)
    owner = expert_ids // local_experts
    column = expert_ids % local_experts
    slot_place = (owner * local_experts + column) * capacity + rank_in_block
    slot_count = num_experts * capacity
    slot_iota = jnp.arange(slot_count, dtype=jnp.int32)
    matched = slot_place[None, :, :] == slot_iota[:, None, None]
    dispatch = jnp.any(matched, axis=2).astype(jnp.bfloat16)
    sent_tokens = jnp.dot(dispatch, tokens, preferred_element_type=jnp.float32).astype(jnp.bfloat16)
    sent_grads = jnp.dot(dispatch, out_grad, preferred_element_type=jnp.float32).astype(
        jnp.bfloat16
    )
    sent_routes = jnp.sum(
        jnp.where(matched, route_weights.astype(jnp.float32)[None], 0.0), axis=(1, 2)
    ).astype(jnp.bfloat16)
    arrived_tokens, arrived_grads, arrived_routes = (
        lax.all_to_all(sent_tokens, "expert", split_axis=0, concat_axis=0, tiled=True),
        lax.all_to_all(sent_grads, "expert", split_axis=0, concat_axis=0, tiled=True),
        lax.all_to_all(sent_routes, "expert", split_axis=0, concat_axis=0, tiled=True),
    )
    token_grid = arrived_tokens.reshape(axis_devices, local_experts, capacity, model_width)
    grad_grid = arrived_grads.reshape(axis_devices, local_experts, capacity, model_width)
    route_grid = arrived_routes.reshape(axis_devices, local_experts, capacity)
    out_blocks = []
    gate_parts = []
    up_parts = []
    down_parts = []
    for slot_id in range(local_experts):
        lower = run_rows(
            token_grid[:half_axis, slot_id].reshape(-1, model_width),
            grad_grid[:half_axis, slot_id].reshape(-1, model_width),
            route_grid[:half_axis, slot_id].reshape(-1),
            gate_weight[slot_id],
            up_weight[slot_id],
            down_weight[slot_id],
        )
        upper = run_rows(
            token_grid[half_axis:, slot_id].reshape(-1, model_width),
            grad_grid[half_axis:, slot_id].reshape(-1, model_width),
            route_grid[half_axis:, slot_id].reshape(-1),
            gate_weight[slot_id],
            up_weight[slot_id],
            down_weight[slot_id],
        )
        out_blocks.append(
            jnp.concatenate(
                [
                    lower[0].reshape(half_axis, capacity, model_width),
                    upper[0].reshape(axis_devices - half_axis, capacity, model_width),
                ],
                axis=0,
            )
        )
        gate_parts.append(lower[1].astype(jnp.float32) + upper[1].astype(jnp.float32))
        up_parts.append(lower[2].astype(jnp.float32) + upper[2].astype(jnp.float32))
        down_parts.append(lower[3].astype(jnp.float32) + upper[3].astype(jnp.float32))
    out_grid = jnp.stack(out_blocks, axis=1).reshape(slot_count, model_width)
    returned_rows = lax.all_to_all(out_grid, "expert", split_axis=0, concat_axis=0, tiled=True)
    grad_input = lax.dot_general(
        dispatch, returned_rows, (((0,), (0,)), ((), ())), preferred_element_type=jnp.float32
    ).astype(jnp.bfloat16)
    summed_gate, summed_up, summed_down = (
        lax.psum_scatter(
            jnp.stack(gate_parts).astype(jnp.bfloat16), "dp", scatter_dimension=1, tiled=True
        ).astype(jnp.float32),
        lax.psum_scatter(
            jnp.stack(up_parts).astype(jnp.bfloat16), "dp", scatter_dimension=1, tiled=True
        ).astype(jnp.float32),
        lax.psum_scatter(
            jnp.stack(down_parts).astype(jnp.bfloat16), "dp", scatter_dimension=1, tiled=True
        ).astype(jnp.float32),
    )
    factor = 1.0 / data_groups
    grad_gate = (summed_gate * factor).astype(jnp.bfloat16)
    grad_up = (summed_up * factor).astype(jnp.bfloat16)
    grad_down = (summed_down * factor).astype(jnp.bfloat16)
    return (grad_input, grad_gate, grad_up, grad_down, expert_load)


def solution(mesh):
    return jax.shard_map(
        shards,
        mesh=mesh,
        in_specs=(
            P(("expert", "dp"), None),
            P(("expert", "dp"), None),
            P(("expert", "dp"), None),
            P(("expert", "dp"), None),
            P("expert", None, None),
            P("expert", None, None),
            P("expert", None, None),
        ),
        out_specs=(
            P(("expert", "dp"), None),
            P("expert", "dp", None),
            P("expert", "dp", None),
            P("expert", "dp", None),
            P(),
        ),
        check_vma=False,
    )
```

profile of v0, /device:TPU:0, one launch (start us, length us, event | category | flops | bytes accessed | tf_op | source)
XLA Modules:
  0.0 581.1 jit_solution(11059658408006949219)
XLA Ops:
  7.2 0.8 convert_reduce_fusion
  7.9 0.7 bitcast_or_fusion
  9.1 7.1 %gather_fusion = s32[1024]{0:T(1024)S(1)} fusion(s32[128,16]{1,0:T(8,128)S(1)} %sub.22, s32[1024]{0:T(1024)S(1)} %reshape.168), kind=kCustom, calls=%fused_computation | custom fusion | bytes 16384 | tf_op jit(solution)/shard_map/jit(take_along_axis)/gather | solution.py:81
  16.4 11.5 %select_reduce_fusion = bf16[1536]{0:T(1024)(128)(2,1)S(1)} fusion(f32[128,8]{0,1:T(8,128)S(1)} %convert_element_type.304, s32[128,8]{0,1:T(8,128)S(1)} %fusion.78), kind=kLoop, calls=%fused_computation.4 | loop fusion | flops 4717056 | bytes 11264 | tf_op jit(solution)/shard_map/reduce_sum | solution.py:93
  27.9 0.7 convert_element_type.408
  28.6 7.3 %all-to-all-start = ((bf16[8,192,1]{1,2,0:T(2,128)(2,1)}), bf16[8,192,1]{1,2,0:T(2,128)(2,1)S(1)}, u32[]{:S(2)}, u32[]{:S(2)}) async-start(bf16[8,192,1]{1,2,0:T(2,128)(2,1)} %convert_element_type.408), calls=%async_computation | async-start | bytes 16384 | tf_op jit(solution)/shard_map/all_to_all | solution.py:99
  35.8 5.6 fusion
  41.4 4.4 convolution_convert_fusion
  45.8 6.4 %all-to-all-start.2 = ((bf16[8,192,2048]{2,1,0:T(8,128)(2,1)}), bf16[8,192,2048]{2,1,0:T(8,128)(2,1)}, u32[]{:S(2)}, u32[]{:S(2)}) async-start(bf16[8,192,2048]{2,1,0:T(8,128)(2,1)} %bitcast.159), calls=%async_computation.2 | async-start | bytes 12582912 | tf_op jit(solution)/shard_map/all_to_all | solution.py:97
  52.2 4.4 convolution_convert_fusion.1
  56.6 133.1 %all-to-all-done.2 = bf16[8,192,2048]{2,1,0:T(8,128)(2,1)} async-done(((bf16[8,192,2048]{2,1,0:T(8,128)(2,1)}), bf16[8,192,2048]{2,1,0:T(8,128)(2,1)}, u32[]{:S(2)}, u32[]{:S(2)}) %all-to-all-start.2) | async-done | bytes 6291488 | tf_op jit(solution)/shard_map/all_to_all | solution.py:97
  189.8 4.8 all-to-all-start.1
  195.1 3.6 fusion.91
  198.9 1.0 fusion.35
  199.9 2.4 copy-done.6
  202.3 1.8 fusion.41
  204.1 1.8 fusion.31
  205.9 1.8 fusion.38
  207.7 1.8 fusion.17
  209.5 1.8 fusion.23
  211.3 1.8 fusion.13
  213.2 1.8 fusion.20
  215.0 116.8 %all-to-all-done.1 = bf16[8,192,2048]{2,1,0:T(8,128)(2,1)} async-done(((bf16[8,192,2048]{2,1,0:T(8,128)(2,1)}), bf16[8,192,2048]{2,1,0:T(8,128)(2,1)}, u32[]{:S(2)}, u32[]{:S(2)}) %all-to-all-start.1) | async-done | bytes 6291488 | tf_op jit(solution)/shard_map/all_to_all | solution.py:98
  331.8 4.3 slice_convert_fusion.3
  336.2 4.0 multiply_convert_fusion.3
  340.2 1.1 multiply_convert_fusion.17
  341.6 1.2 convolution_convert_fusion.12
  342.8 2.3 convolution_convert_fusion.13
  345.5 2.2 convolution_convert_fusion.11
  347.7 1.1 multiply_convert_fusion.15
  349.1 2.4 convolution_convert_fusion.10
  351.5 1.2 convolution_convert_fusion.9
  352.7 2.2 convolution_convert_fusion.8
  354.9 1.1 multiply_convert_fusion.13
  356.3 1.2 convolution_convert_fusion.6
  357.5 2.4 convolution_convert_fusion.7
  360.5 2.2 convolution_convert_fusion.5
  362.7 1.1 multiply_convert_fusion.11
  363.8 1.2 convolution_convert_fusion.3
  365.1 2.3 convolution_convert_fusion.4
  367.4 2.3 convolution_convert_fusion.2
  370.5 2.0 pad_maximum_fusion.2
  372.5 1.3 copy-done.18
  373.9 2.0 fusion.5
  376.6 2.0 pad_maximum_fusion.1
  378.6 2.8 fusion.15
  381.8 2.7 fusion.11
  384.5 2.7 fusion.33
  387.1 1.0 add_convert_fusion.7
  388.2 2.8 fusion.29
  391.1 2.6 add_convert_fusion.6
  393.7 0.7 copy-done.8
  394.4 1.0 add_convert_fusion.9
  395.5 1.0 add_convert_fusion.8
  397.1 3.2 pad_maximum_fusion
  400.3 4.9 all-to-all-start.3
  405.2 2.2 fusion.9
  407.6 0.6 fusion.10
  408.2 2.0 pad_maximum_fusion.3
  410.4 152.3 %psum.7 = f32[16]{0:T(128)S(1)} all-reduce(f32[16]{0:T(128)S(1)} %select_reduce_fusion.1), channel_id=1, replica_groups=mesh['expert'=8,'dp'=4] {'expert','dp'}, use_global_device_ids=true, to_apply=%region_8.9 | all-reduce | flops 16 | bytes 128 | tf_op jit(solution)/shard_map/psum | solution.py:76
  563.2 2.2 multiply_convert_fusion.5
  565.4 2.2 multiply_convert_fusion.6
  567.5 2.2 multiply_convert_fusion.4
  569.7 4.7 convolution_convert_fusion.14
  (109 shorter events, 6.7 us)
Async XLA Ops:
  7.2 34.2 %copy-start = (bf16[128,2048]{1,0:T(8,128)(2,1)S(1)}, bf16[128,2048]{1,0:T(8,128)(2,1)}, u32[]{:S(2)}) copy-start(bf16[128,2048]{1,0:T(8,128)(2,1)} %param.7) | copy-start | bytes 1572868
  9.1 7.2 %copy-start.28 = (s32[128,8]{0,1:T(8,128)S(1)}, s32[128,8]{0,1:T(8,128)}, u32[]{:S(2)}) copy-start(s32[128,8]{0,1:T(8,128)} %param.10) | copy-start | bytes 12292
  9.1 7.3 %copy-start.29 = (bf16[128,8]{0,1:T(8,128)(2,1)S(1)}, bf16[128,8]{0,1:T(8,128)(2,1)}, u32[]{:S(2)}) copy-start(bf16[128,8]{0,1:T(8,128)(2,1)} %param.9) | copy-start | bytes 6148
  28.6 17.2 %all-to-all-start = ((bf16[8,192,1]{1,2,0:T(2,128)(2,1)}), bf16[8,192,1]{1,2,0:T(2,128)(2,1)S(1)}, u32[]{:S(2)}, u32[]{:S(2)}) async-start(bf16[8,192,1]{1,2,0:T(2,128)(2,1)} %convert_element_type.408), calls=%async_computation | async-start | bytes 16384 | tf_op jit(solution)/shard_map/all_to_all | solution.py:99
  45.8 6.4 %copy-start.21 = (bf16[128,2048]{1,0:T(8,128)(2,1)S(1)}, bf16[128,2048]{1,0:T(8,128)(2,1)}, u32[]{:S(2)}) copy-start(bf16[128,2048]{1,0:T(8,128)(2,1)} %param.8) | copy-start | bytes 1572868
  45.8 144.0 %all-to-all-start.2 = ((bf16[8,192,2048]{2,1,0:T(8,128)(2,1)}), bf16[8,192,2048]{2,1,0:T(8,128)(2,1)}, u32[]{:S(2)}, u32[]{:S(2)}) async-start(bf16[8,192,2048]{2,1,0:T(8,128)(2,1)} %bitcast.159), calls=%async_computation.2 | async-start | bytes 12582912 | tf_op jit(solution)/shard_map/all_to_all | solution.py:97
  189.8 142.1 %all-to-all-start.1 = ((bf16[8,192,2048]{2,1,0:T(8,128)(2,1)}), bf16[8,192,2048]{2,1,0:T(8,128)(2,1)}, u32[]{:S(2)}, u32[]{:S(2)}) async-start(bf16[8,192,2048]{2,1,0:T(8,128)(2,1)} %bitcast.158), calls=%async_computation.1 | async-start | bytes 12582912 | tf_op jit(solution)/shard_map/all_to_all | solution.py:98
  194.5 368.7 %reduce-scatter.6.cloned.1.call-start = ((), (), s32[]{:S(2)}) async-start(), calls=%async_computation.8 | async-start | bytes 3932160 | tf_op jit(solution)/shard_map/reduce_scatter | solution.py:146
  195.1 3.8 copy-start.2
  198.7 1.2 copy-start.13
  198.7 7.2 %copy-start.11 = (bf16[4,1,96,2048]{3,2,1,0:T(8,128)(2,1)}, bf16[4,1,96,2048]{3,2,1,0:T(8,128)(2,1)S(1)}, u32[]{:S(2)}) copy-start(bf16[4,1,96,2048]{3,2,1,0:T(8,128)(2,1)S(1)} %get-tuple-element.44) | copy-start | bytes 4718596
  198.7 10.8 %copy-start.9 = (bf16[4,1,96,2048]{3,2,1,0:T(8,128)(2,1)}, bf16[4,1,96,2048]{3,2,1,0:T(8,128)(2,1)S(1)}, u32[]{:S(2)}) copy-start(bf16[4,1,96,2048]{3,2,1,0:T(8,128)(2,1)S(1)} %get-tuple-element.43) | copy-start | bytes 4718596
  198.9 3.5 copy-start.6
  336.1 4.0 copy-start.30
  336.2 4.0 copy-start.37
  340.2 1.4 copy-start.14
  345.5 2.2 copy-start.35
  345.5 2.2 copy-start.36
  347.7 1.4 copy-start.12
  352.7 2.3 copy-start.33
  352.7 2.2 copy-start.34
  354.9 1.4 copy-start.10
  356.1 1.5 copy-start.22
  360.5 2.2 copy-start.31
  360.5 2.2 copy-start.32
  363.8 1.2 copy-start.24
  363.8 1.2 copy-start.26
  372.5 1.4 copy-start.18
  372.5 192.9 %reduce-scatter.4.cloned.1.call-start = ((), (), s32[]{:S(2)}) async-start(), calls=%async_computation.7 | async-start | bytes 3932160 | tf_op jit(solution)/shard_map/reduce_scatter | solution.py:143
  373.9 2.0 copy-start.19
  373.9 2.4 copy-start.20
  376.6 2.0 copy-start.23
  378.6 3.1 copy-start.3
  378.6 3.1 copy-start.27
  384.5 2.7 copy-start.7
  388.2 2.9 copy-start.5
  388.2 2.9 copy-start.25
  391.1 2.6 copy-start.4
  391.1 3.3 copy-start.8
  400.3 4.9 copy-start.15
  400.3 169.4 %all-to-all-start.3 = ((bf16[8,192,2048]{2,1,0:T(8,128)(2,1)}), bf16[8,192,2048]{2,1,0:T(8,128)(2,1)}, u32[]{:S(2)}, u32[]{:S(2)}) async-start(bf16[8,192,2048]{2,1,0:T(8,128)(2,1)} %bitcast.160), calls=%async_computation.3 | async-start | bytes 12582912 | tf_op jit(solution)/shard_map/all_to_all | solution.py:138
  405.2 162.4 %reduce-scatter.8.cloned.1.call-start = ((), (), s32[]{:S(2)}) async-start(), calls=%async_computation.9 | async-start | bytes 3932160 | tf_op jit(solution)/shard_map/reduce_scatter | solution.py:149
  405.2 2.2 copy-start.16
  405.2 2.4 copy-start.17
  569.7 4.7 copy-start.1
Sparse Core Ops, SparseCore 0:
  372.6 37.0 reduce-scatter.5
  412.4 37.9 reduce-scatter.3
  452.9 37.9 reduce-scatter.7
where the time goes:
time: 589 us; the launch traced here: 581 us
  waiting for transfers between devices  250 us (42%)
  blocking collectives  152 us (26%)
  matrix products  71.3 us (12%)
  other arithmetic  50.8 us (9%)
  starting transfers between devices  23.4 us (4%)
  local copies, waits for them, and re-layouts  18.7 us (3%)
  between operations  14.5 us (2%)
    psum x1, blocking collectives, shards(): lax.psum((local_count, local_weight), ('expert', 'dp'))  152 us
    all_to_all x1, waiting for transfers between devices, shards(): lax.all_to_all(sent_tokens, 'expert', split_axis=0, concat_axis=0, tiled=...  133 us
    all_to_all x1, waiting for transfers between devices, shards(): lax.all_to_all(sent_grads, 'expert', split_axis=0, concat_axis=0, tiled=T...  117 us
  transfers between devices with their start and end apart: 7, of which 2 were waited for; matrix products, arithmetic and copies ran while one was open for 12% of the time, Pallas kernels for 0%

commit v1 on v0

v1 whole, which is shorter than its diff:
```python
import jax
import jax.numpy as jnp
from jax import lax
from jax.sharding import PartitionSpec as P

BF = jnp.bfloat16
F32 = jnp.float32
LANES = 128


def dot(a, b, ca, cb):
    return lax.dot_general(a, b, (((ca,), (cb,)), ((), ())), preferred_element_type=F32)


def tie(*values):
    return lax.optimization_barrier(values)


def shards(tokens, out_grad, route_weights, expert_ids, gate_weight, up_weight, down_weight):
    local_experts, width, hidden = gate_weight.shape
    devices = lax.axis_size("expert")
    groups = lax.axis_size("dp")
    num_experts = local_experts * devices
    rows, top_count = expert_ids.shape
    outer = devices // 2
    inner_width = local_experts * hidden
    me = lax.axis_index("expert")
    my_group = lax.axis_index("dp")

    def ring(value, step):
        pairs = [(2 * z + x, 2 * ((z + step) % outer) + x) for z in range(outer) for x in range(2)]
        return lax.ppermute(value, "expert", pairs)

    def cross(value):
        return lax.ppermute(value, "expert", [(i, i ^ 1) for i in range(devices)])

    def swap(value, bit):
        return lax.ppermute(value, "dp", [(i, i ^ bit) for i in range(groups)])

    lanes = jnp.arange(LANES, dtype=jnp.int32)
    dense = jnp.sum(
        jnp.where(
            expert_ids[:, :, None] == lanes, route_weights.astype(F32)[:, :, None], 0.0
        ),
        axis=1,
    ).astype(BF)
    grads = jnp.concatenate([out_grad, dense], axis=1)

    gate_up = jnp.concatenate(
        [gate_weight[e] for e in range(local_experts)] + [up_weight[e] for e in range(local_experts)],
        axis=1,
    )
    down = down_weight.reshape(inner_width, width)

    def forward(token_rows):
        linear = dot(token_rows, gate_up, 1, 0)
        return linear

    def backward(linear, grad_rows):
        cotangent = grad_rows[:, :width]
        routes = grad_rows[:, width:].astype(F32)
        weight = jnp.concatenate(
            [
                jnp.broadcast_to(
                    jnp.sum(
                        jnp.where(lanes == me * local_experts + e, routes, 0.0), axis=1, keepdims=True
                    ),
                    (grad_rows.shape[0], hidden),
                )
                for e in range(local_experts)
            ],
            axis=1,
        )
        gate_linear = linear[:, :inner_width]
        up_linear = linear[:, inner_width:]
        delta_hidden = weight * dot(cotangent, down, 1, 1)
        logistic = jax.nn.sigmoid(gate_linear)
        activated = gate_linear * logistic
        scaled_hidden = (weight * activated * up_linear).astype(BF)
        delta_gate = delta_hidden * up_linear * logistic * (1.0 + gate_linear * (1.0 - logistic))
        delta_up = delta_hidden * activated
        delta = jnp.concatenate([delta_gate.astype(BF), delta_up.astype(BF)], axis=1)
        partial = dot(delta, gate_up, 1, 1).astype(BF)
        return partial, delta, scaled_hidden, cotangent

    token_now, grad_now = tokens, grads
    token_cross, grad_cross = None, None
    first_grad_cross = None
    results = []
    flying_a = (ring(token_now, 1), cross(token_now))
    flying_b = (ring(grad_now, 1), cross(grad_now))
    held = ()
    for step in range(outer + 1):
        token_rows = [t for t in (token_now, token_cross) if t is not None]
        token_block = token_rows[0] if len(token_rows) == 1 else jnp.concatenate(token_rows, axis=0)
        linear = forward(token_block)
        if step > 0:
            got = tie(*flying_b, linear)
            linear = got[-1]
            if step < outer:
                grad_now, grad_cross = got[0], got[1]
                if step == 1:
                    first_grad_cross = grad_cross
                if step < outer - 1:
                    flying_b = (ring(grad_now, 1), cross(grad_now))
                else:
                    flying_b = (ring(first_grad_cross, outer - 1),)
            else:
                grad_now, grad_cross = None, got[0]
        grad_rows = [g for g in (grad_now, grad_cross) if g is not None]
        grad_block = grad_rows[0] if len(grad_rows) == 1 else jnp.concatenate(grad_rows, axis=0)
        result = backward(linear, grad_block)
        results.append((token_block, grad_block) + result)
        if step < outer:
            got = tie(*flying_a, *result)
            results[-1] = (token_block, grad_block) + tuple(got[-4:])
            if step < outer - 1:
                token_now, token_cross = got[0], got[1]
                if step + 1 < outer - 1:
                    flying_a = (ring(token_now, 1), cross(token_now))
                else:
                    flying_a = (cross(token_now),)
            else:
                token_now, token_cross = None, got[0]

    own = [results[s][2][:rows] for s in range(outer)]
    other = [results[s + 1][2][-rows:] for s in range(outer)]
    order = [s for s in range(outer - 1, 0, -1)] + [0]
    total = None
    for s in order:
        both = own[s].astype(F32) + cross(other[s]).astype(F32)
        if s:
            both = ring(both.astype(BF), outer - s).astype(F32)
        total = both if total is None else total + both
    grad_input = total.astype(BF)

    load = sum(
        jnp.sum(r[1][:, width:].astype(F32), axis=0, keepdims=True) for r in results
    )
    bit = 1
    while bit < groups:
        load = load + swap(load, bit)
        bit *= 2
    expert_load = load[0, :num_experts] * (num_experts / (rows * devices * groups * top_count))

    all_tokens = jnp.concatenate([r[0] for r in results], axis=0)
    all_delta = jnp.concatenate([r[3] for r in results], axis=0)
    all_hidden = jnp.concatenate([r[4] for r in results], axis=0)
    all_cotangent = jnp.concatenate([r[5] for r in results], axis=0)
    grad_gate_up = dot(all_tokens, all_delta, 0, 0).astype(BF)
    grad_down = dot(all_hidden, all_cotangent, 0, 0).astype(BF)

    def reduce_groups(value):
        bit = 1
        size = groups
        index = my_group
        while size > 1:
            value = value.reshape((size // 2, 2) + value.shape[1:])
            low = index % 2
            mine = lax.dynamic_index_in_dim(value, low, 1, keepdims=False)
            theirs = lax.dynamic_index_in_dim(value, 1 - low, 1, keepdims=False)
            summed = mine.astype(F32) + swap(theirs, bit).astype(F32)
            size //= 2
            index = index // 2
            bit *= 2
            value = summed.astype(BF) if size > 1 else summed
        return value[0] * (1.0 / groups)

    mine = reduce_groups(grad_gate_up.reshape(groups, width // groups, 2 * inner_width)).astype(BF)
    mine = mine.reshape(width // groups, 2, local_experts, hidden)
    out_gate = mine[:, 0].transpose(1, 0, 2)
    out_up = mine[:, 1].transpose(1, 0, 2)
    down_chunks = grad_down.reshape(local_experts, groups, hidden // groups, width).transpose(1, 0, 2, 3)
    out_down = reduce_groups(down_chunks).astype(BF)
    return (grad_input, out_gate, out_up, out_down, expert_load)


def solution(mesh):
    return jax.shard_map(
        shards,
        mesh=mesh,
        in_specs=(
            P(("expert", "dp"), None),
            P(("expert", "dp"), None),
            P(("expert", "dp"), None),
            P(("expert", "dp"), None),
            P("expert", None, None),
            P("expert", None, None),
            P("expert", None, None),
        ),
        out_specs=(
            P(("expert", "dp"), None),
            P("expert", "dp", None),
            P("expert", "dp", None),
            P("expert", "dp", None),
            P(),
        ),
        check_vma=False,
    )
```

time: 589 us -> 237 us (0.40); the launches traced: 581 us -> 236 us
  waiting for transfers between devices: 250 us -> 72.9 us
  blocking collectives: 152 us -> 0 us
  local copies, waits for them, and re-layouts: 18.7 us -> 50.5 us
  other arithmetic: 50.8 us -> 25.5 us
  matrix products: 71.3 us -> 48.6 us
  starting transfers between devices: 23.4 us -> 37.2 us
  between operations: 14.5 us -> 1.46 us
    all_to_all x4 -> x0, waiting for transfers between devices: 250 us -> none  [the longest x1 133 us: shards(): lax.all_to_all(sent_tokens, 'expert', split_axis=0, concat_axis=0, tiled=...]
    psum x1 -> x0, blocking collectives: 152 us -> none  [shards(): lax.psum((local_count, local_weight), ('expert', 'dp'))]
    ppermute x0 -> x27, waiting for transfers between devices: none -> 72.9 us  [the longest x6 45 us: swap(): return lax.ppermute(value, 'dp', [(i, i ^ bit) for i in range(groups)])]
    ppermute x0 -> x27, starting transfers between devices: none -> 37.2 us  [the longest x10 21 us: ring(): return lax.ppermute(value, 'expert', pairs)]
    all_to_all x4 -> x0, starting transfers between devices: 23.2 us -> none  [the longest x1 7.25 us: shards(): lax.all_to_all(sent_routes, 'expert', split_axis=0, concat_axis=0, tiled=...]
    dot_general x35 -> x17, matrix products: 71.3 us -> 48.6 us  [dot(): lax.dot_general(a, b, (((ca,), (cb,)), ((), ())), preferred_element_type=...]
    unnamed x76 -> x84, local copies, waits for them, and re-layouts: 6.51 us -> 26.1 us
    another operation x12 -> x0, other arithmetic: 15.9 us -> none  [the longest x3 4.77 us: shards(): jnp.stack(down_parts).astype(jnp.bfloat16)]
  transfers between devices with their start and end apart: 7 -> 27, of which waited for: 2 -> 7; matrix products, arithmetic and copies ran while one was open for 12% -> 47% of each run, Pallas kernels for 0% -> 0%
where the time goes in v1:
time: 237 us; the launch traced here: 236 us
  waiting for transfers between devices  72.9 us (31%)
  local copies, waits for them, and re-layouts  50.5 us (21%)
  matrix products  48.6 us (21%)
  starting transfers between devices  37.2 us (16%)
  other arithmetic  25.5 us (11%)
    dot_general x17, matrix products, dot(): lax.dot_general(a, b, (((ca,), (cb,)), ((), ())), preferred_element_type=...  48.6 us
    ppermute x6, waiting for transfers between devices, swap(): return lax.ppermute(value, 'dp', [(i, i ^ bit) for i in range(groups)])  45 us
    unnamed x84, local copies, waits for them, and re-layouts  26.1 us
    ppermute x10, starting transfers between devices, ring(): return lax.ppermute(value, 'expert', pairs)  21 us
    ppermute x10, waiting for transfers between devices, ring(): return lax.ppermute(value, 'expert', pairs)  17 us
    ppermute x11, waiting for transfers between devices, cross(): return lax.ppermute(value, 'expert', [(i, i ^ 1) for i in range(devices)])  10.9 us
    ppermute x11, starting transfers between devices, cross(): return lax.ppermute(value, 'expert', [(i, i ^ 1) for i in range(devices)])  10.9 us
    convert_element_type x3, other arithmetic, shards(): both = ring(both.astype(BF), outer - s).astype(F32)  6.82 us
  transfers between devices with their start and end apart: 27, of which 7 were waited for; matrix products, arithmetic and copies ran while one was open for 47% of the time, Pallas kernels for 0%

profile of v1, /device:TPU:0, one launch (start us, length us, event | category | flops | bytes accessed | tf_op | source)
XLA Modules:
  0.0 236.1 jit_solution(8699853190982942598)
XLA Ops:
  0.6 3.1 %collective-permute-start = (bf16[128,2048]{1,0:T(8,128)(2,1)}, bf16[128,2048]{1,0:T(8,128)(2,1)}, u32[]{:S(2)}, u32[]{:S(2)}) collective-permute-start(bf16[128,2048]{1,0:T(8,128)(2,1)} %param.7), channel_id=1, source_target_pairs={{0,8},{4,12},{8,16},{12,20},{16,24},{20,28},{24,0},{28,4},{1,9},{5... | collective-permute-start | bytes 1572872 | tf_op jit(solution)/shard_map/ppermute | solution.py:32
  3.7 1.5 collective-permute-start.1
  7.1 1.9 pad_maximum_fusion.7
  9.0 1.6 collective-permute-start.4
  11.2 1.9 constant_dynamic-update-slice_fusion.13
  13.0 3.5 %slice_bitcast_fusion.1 = (bf16[2048,384]{1,0:T(8,128)(2,1)S(1)}, bf16[2048,384]{1,0:T(8,128)(2,1)S(1)}, bf16[2048,384]{1,0:T(8,128)(2,1)S(1)}, bf16[2048,384]{1,0:T(8,128)(2,1)S(1)}) fusion(bf16[2,2048,384]{2,1,0:T(8,128)(2,1)} %param.12, bf16[2,2048,384]{2,1,0:T(8,128)(2,1)} %param.11), kind=kLoop, calls=%fused_computation.17 | loop fusion | bytes 12582912 | tf_op jit(solution)/shard_map/squeeze | solution.py:50
  17.3 2.7 %copy-done.1 = bf16[2048,1536]{1,0:T(8,128)(2,1)} copy-done((bf16[2048,1536]{1,0:T(8,128)(2,1)}, bf16[2048,1536]{1,0:T(8,128)(2,1)S(1)}, u32[]{:S(2)}) %copy-start.1) | copy-done | bytes 6291480
  19.9 1.9 convolution_bitcast_fusion
  22.1 3.2 %multiply_convert_fusion.11 = (bf16[128,768]{1,0:T(8,128)(2,1)S(1)}, bf16[128,768]{1,0:T(8,128)(2,1)S(1)}, bf16[128,768]{1,0:T(8,128)(2,1)}) fusion(f32[128,1536]{1,0:T(8,128)} %convolution_bitcast_fusion, f32[128,384]{1,0:T(8,128)S(1)} %broadcast_in_dim.122, f32[128,384]{1,0:T(8,128)S(1)} %broadcast_in_dim.120, bf16[128,2048]{1,0:T(8,128)(2,1)} %param.8, ...), kind=kOutput, calls=%fused_computation.91 | convolution fusion | flops 404422656 | bytes 5439488 | tf_op jit(solution)/shard_map/dot_general | solution.py:12
  26.2 6.1 %convolution_convert_fusion.6 = bf16[128,2048]{1,0:T(8,128)(2,1)} fusion(bf16[2048,1536]{1,0:T(8,128)(2,1)} %copy-done.1, bf16[128,768]{1,0:T(8,128)(2,1)} %copy-done.16, bf16[128,768]{1,0:T(8,128)(2,1)} %copy-done.15), kind=kOutput, calls=%fused_computation.13 | convolution fusion | flops 806354944 | bytes 7208960 | tf_op jit(solution)/shard_map/dot_general | solution.py:12
  32.3 1.6 collective-permute-start.2
  33.9 1.5 collective-permute-start.3
  35.4 1.1 constant_dynamic-update-slice_fusion.12
  36.6 1.1 constant_dynamic-update-slice_fusion.11
  37.7 4.9 %fusion.2 = f32[256,1536]{1,0:T(8,128)S(1)} fusion(bf16[2048,1536]{1,0:T(8,128)(2,1)} %copy-done.1, bf16[128,2048]{1,0:T(8,128)(2,1)} %collective-permute-done.1, bf16[128,2048]{1,0:T(8,128)(2,1)} %collective-permute-done), kind=kOutput, calls=%fused_computation.25 | convolution fusion | flops 1612709888 | bytes 8912896 | tf_op jit(solution)/shard_map/dot_general | solution.py:12
  42.6 1.1 constant_dynamic-update-slice_fusion.1
  43.7 1.1 constant_dynamic-update-slice_fusion
  46.0 3.5 %collective-permute-start.13 = (bf16[128,2176]{1,0:T(8,128)(2,1)}, bf16[128,2176]{1,0:T(8,128)(2,1)S(1)}, u32[]{:S(2)}, u32[]{:S(2)}) collective-permute-start(bf16[128,2176]{1,0:T(8,128)(2,1)} %collective-permute-done.5), channel_id=1, source_target_pairs={{0,24},{4,28},{8,0},{12,4},{16,8},{20,12},{24,16},{28,20},{1,25},{... | collective-permute-start | bytes 1671176 | tf_op jit(solution)/shard_map/ppermute | solution.py:32
  49.7 1.4 multiply_convert_fusion.7
  52.4 1.8 convolution_convert_fusion.4
  54.3 1.6 collective-permute-start.7
  57.0 1.8 fusion.6
  58.8 3.9 %collective-permute-done.8 = bf16[128,2176]{1,0:T(8,128)(2,1)S(1)} collective-permute-done((bf16[128,2176]{1,0:T(8,128)(2,1)}, bf16[128,2176]{1,0:T(8,128)(2,1)S(1)}, u32[]{:S(2)}, u32[]{:S(2)}) %collective-permute-start.8) | collective-permute-done | bytes 557088 | tf_op jit(solution)/shard_map/ppermute | solution.py:32
  64.0 9.2 %collective-permute-start.11 = (bf16[128,2176]{1,0:T(8,128)(2,1)S(1)}, bf16[128,2176]{1,0:T(8,128)(2,1)S(1)}, u32[]{:S(2)}, u32[]{:S(2)}) collective-permute-start(bf16[128,2176]{1,0:T(8,128)(2,1)S(1)} %collective-permute-done.8), channel_id=1, source_target_pairs={{0,8},{4,12},{8,16},{12,20},{16,24},{20,28},{24,0},{28,4},{1,9},{5... | collective-permute-start | bytes 1671176 | tf_op jit(solution)/shard_map/ppermute | solution.py:32
  73.5 1.4 multiply_convert_fusion.5
  74.9 1.8 convolution_convert_fusion.3
  76.7 9.2 %collective-permute-done.6 = bf16[128,2048]{1,0:T(8,128)(2,1)S(1)} collective-permute-done((bf16[128,2048]{1,0:T(8,128)(2,1)S(1)}, bf16[128,2048]{1,0:T(8,128)(2,1)S(1)}, u32[]{:S(2)}, u32[]{:S(2)}) %collective-permute-start.6) | collective-permute-done | bytes 524320 | tf_op jit(solution)/shard_map/ppermute | solution.py:32
  86.4 1.5 collective-permute-start.10
  89.2 1.8 fusion.10
  91.0 4.0 %collective-permute-done.11 = bf16[128,2176]{1,0:T(8,128)(2,1)S(1)} collective-permute-done((bf16[128,2176]{1,0:T(8,128)(2,1)S(1)}, bf16[128,2176]{1,0:T(8,128)(2,1)S(1)}, u32[]{:S(2)}, u32[]{:S(2)}) %collective-permute-start.11) | collective-permute-done | bytes 557088 | tf_op jit(solution)/shard_map/ppermute | solution.py:32
  95.5 5.9 %collective-permute-done.12 = bf16[128,2176]{1,0:T(8,128)(2,1)S(1)} collective-permute-done((bf16[128,2176]{1,0:T(8,128)(2,1)S(1)}, bf16[128,2176]{1,0:T(8,128)(2,1)S(1)}, u32[]{:S(2)}, u32[]{:S(2)}) %collective-permute-start.12) | collective-permute-done | bytes 557088 | tf_op jit(solution)/shard_map/ppermute | solution.py:35
  102.4 2.1 multiply_convert_fusion.3
  104.5 1.8 convolution_convert_fusion.2
  106.4 1.3 slice.135
  107.7 5.0 %collective-permute-done.10 = bf16[128,2048]{1,0:T(8,128)(2,1)S(1)} collective-permute-done((bf16[128,2048]{1,0:T(8,128)(2,1)S(1)}, bf16[128,2048]{1,0:T(8,128)(2,1)S(1)}, u32[]{:S(2)}, u32[]{:S(2)}) %collective-permute-start.10) | collective-permute-done | bytes 524320 | tf_op jit(solution)/shard_map/ppermute | solution.py:35
  115.9 1.2 multiply_convert_fusion.9
  117.1 2.9 %convolution_convert_fusion.5 = bf16[128,2048]{1,0:T(8,128)(2,1)} fusion(bf16[2048,1536]{1,0:T(8,128)(2,1)S(1)} %bitcast.68, bf16[128,768]{1,0:T(8,128)(2,1)S(1)} %get-tuple-element.116, bf16[128,768]{1,0:T(8,128)(2,1)S(1)} %get-tuple-element.115), kind=kOutput, calls=%fused_computation.12 | convolution fusion | flops 806354944 | bytes 7208960 | tf_op jit(solution)/shard_map/dot_general | solution.py:12
  120.1 1.5 collective-permute-start.14
  121.7 7.6 %convolution_convert_fusion = bf16[2048,1536]{1,0:T(8,128)(2,1)S(1)} fusion(bf16[1024,2048]{1,0:T(8,128)(2,1)S(1)} %constant_dynamic-update-slice_fusion.6, bf16[1024,1536]{1,0:T(8,128)(2,1)S(1)} %fusion.36), kind=kOutput, calls=%fused_computation | convolution fusion | flops 6445596672 | bytes 13631488 | tf_op jit(solution)/shard_map/dot_general | solution.py:12
  129.4 3.1 %constant_dynamic-slice_fusion.3 = (bf16[2,1,512,1536]{3,2,1,0:T(8,128)(2,1)}, bf16[2,1,512,1536]{3,2,1,0:T(8,128)(2,1)}) fusion(bf16[2,2,512,1536]{3,2,1,0:T(8,128)(2,1)S(1)} %bitcast.71, s32[]{:T(128)S(6)} %select_n.88, s32[]{:T(128)S(6)} %select_n.89), kind=kLoop, calls=%fused_computation.150 | loop fusion | bytes 12582920 | tf_op jit(solution)/shard_map/jit(dynamic_index_in_dim)/dynamic_slice | solution.py:160
  132.5 4.7 %copy.27 = bf16[2,1,512,1536]{2,3,0,1:T(8,128)(2,1)} copy(bf16[2,1,512,1536]{3,2,1,0:T(8,128)(2,1)} %get-tuple-element.99) | data formatting | bytes 6291456 | tf_op jit(solution)/shard_map/jit(dynamic_index_in_dim)/dynamic_slice | solution.py:161
  137.2 1.8 constant_dynamic-update-slice_fusion.18
  139.0 1.9 fusion.37
  140.9 2.4 %constant_dynamic-update-slice_fusion.22 = bf16[1024,2048]{1,0:T(8,128)(2,1)} fusion(bf16[1024,2048]{1,0:T(8,128)(2,1)} %copy-done.21, bf16[256,2048]{1,0:T(8,128)(2,1)} %slice.135), kind=kLoop, calls=%fused_computation.143 | loop fusion | bytes 2097152
  144.2 5.9 %convolution_convert_fusion.1 = bf16[768,2048]{1,0:T(8,128)(2,1)S(1)} fusion(bf16[1024,768]{1,0:T(8,128)(2,1)S(1)} %copy-done.23, bf16[1024,2048]{1,0:T(8,128)(2,1)} %slice_dynamic-update-slice_fusion), kind=kOutput, calls=%fused_computation.4 | convolution fusion | flops 3222798336 | bytes 8912896 | tf_op jit(solution)/shard_map/dot_general | solution.py:12
  151.4 2.2 add_convert_fusion.1
  153.6 1.3 dynamic-slice_bitcast_fusion
  155.0 4.7 %copy.32 = bf16[2,1,512,1536]{2,3,0,1:T(8,128)(2,1)} copy(bf16[2,1,512,1536]{3,2,1,0:T(8,128)(2,1)} %get-tuple-element.98) | data formatting | bytes 6291456
  160.3 2.5 %add_convert_fusion.2 = bf16[128,2048]{1,0:T(8,128)(2,1)} fusion(bf16[128,2048]{1,0:T(8,128)(2,1)} %collective-permute-done.16, bf16[256,2048]{1,0:T(8,128)(2,1)} %copy-done.13), kind=kLoop, calls=%fused_computation.39 | loop fusion | flops 1048576 | bytes 1572864 | tf_op jit(solution)/shard_map/convert_element_type | solution.py:133
  162.7 2.1 add_convert_fusion.3
  164.8 1.3 collective-permute-start.15
  166.1 2.8 %fusion = bf16[2,512,1536]{1,2,0:T(8,128)(2,1)S(1)} fusion(bf16[2,512,1536]{1,2,0:T(8,128)(2,1)} %collective-permute-done.21, bf16[2,1,512,1536]{2,3,0,1:T(8,128)(2,1)S(1)} %copy-done.6), kind=kLoop, calls=%fused_computation.3 | loop fusion | flops 6291456 | bytes 9437184 | tf_op jit(solution)/shard_map/convert_element_type | solution.py:166
  168.9 1.2 constant_dynamic-slice_fusion.1
  170.2 1.5 collective-permute-start.22
  173.1 1.6 collective-permute-start.26
  175.7 31.2 %collective-permute-done.26 = f32[1,128]{1,0:T(1,128)S(1)} collective-permute-done((f32[1,128]{1,0:T(1,128)S(1)}, f32[1,128]{1,0:T(1,128)S(1)}, u32[]{:S(2)}, u32[]{:S(2)}) %collective-permute-start.26) | collective-permute-done | bytes 544 | tf_op jit(solution)/shard_map/ppermute | solution.py:38
  206.9 1.5 collective-permute-start.24
  208.9 3.2 %add_convert_fusion = bf16[128,2048]{1,0:T(8,128)(2,1)} fusion(bf16[128,2048]{1,0:T(8,128)(2,1)} %collective-permute-done.20, bf16[128,2048]{1,0:T(8,128)(2,1)} %convolution_convert_fusion.6, bf16[128,2048]{1,0:T(8,128)(2,1)} %collective-permute-done.19, bf16[128,2048]{1,0:T(8,128)(2,1)} %collective-permute-done.17, bf16[128,2048]{1,0:T(8,128)(2,1)} %collective-permute-done.15), kind=kLoop, calls=%fused_computation.37 | loop fusion | flops 2621440 | bytes 3145728 | tf_op jit(solution)/shard_map/convert_element_type | solution.py:135
  212.1 13.8 %collective-permute-done.24 = bf16[1,2,96,2048]{3,2,1,0:T(8,128)(2,1)} collective-permute-done((bf16[1,2,96,2048]{3,2,1,0:T(8,128)(2,1)}, bf16[1,2,96,2048]{3,2,1,0:T(8,128)(2,1)}, u32[]{:S(2)}, u32[]{:S(2)}) %collective-permute-start.24) | collective-permute-done | bytes 786464 | tf_op jit(solution)/shard_map/ppermute | solution.py:38
  225.8 2.5 %fusion.14 = bf16[2,96,2048]{2,1,0:T(8,128)(2,1)} fusion(bf16[1,2,96,2048]{3,2,1,0:T(8,128)(2,1)} %collective-permute-done.24, bf16[2,2,96,2048]{3,2,1,0:T(8,128)(2,1)} %copy-done.7, s32[]{:T(128)S(6)} %select_n.92), kind=kLoop, calls=%fused_computation.41 | loop fusion | flops 1966080 | bytes 2359300 | tf_op jit(solution)/shard_map/convert_element_type | solution.py:174
  228.4 1.9 multiply_convert_fusion
  230.3 1.2 slice_bitcast_fusion.4
  231.5 2.3 copy.29
  233.8 2.3 copy.30
  (149 shorter events, 21.9 us)
Async XLA Ops:
  0.6 21.5 %copy-start = (bf16[2,384,2048]{2,1,0:T(8,128)(2,1)S(1)}, bf16[2,384,2048]{2,1,0:T(8,128)(2,1)}, u32[]{:S(2)}) copy-start(bf16[2,384,2048]{2,1,0:T(8,128)(2,1)} %param.13) | copy-start | bytes 9437188
  0.6 31.6 %collective-permute-start = (bf16[128,2048]{1,0:T(8,128)(2,1)}, bf16[128,2048]{1,0:T(8,128)(2,1)}, u32[]{:S(2)}, u32[]{:S(2)}) collective-permute-start(bf16[128,2048]{1,0:T(8,128)(2,1)} %param.7), channel_id=1, source_target_pairs={{0,8},{4,12},{8,16},{12,20},{16,24},{20,28},{24,0},{28,4},{1,9},{5... | collective-permute-start | bytes 1572872 | tf_op jit(solution)/shard_map/ppermute | solution.py:32
  3.7 28.5 %collective-permute-start.1 = (bf16[128,2048]{1,0:T(8,128)(2,1)}, bf16[128,2048]{1,0:T(8,128)(2,1)}, u32[]{:S(2)}, u32[]{:S(2)}) collective-permute-start(bf16[128,2048]{1,0:T(8,128)(2,1)} %param.7), channel_id=1, source_target_pairs={{0,4},{4,0},{8,12},{12,8},{16,20},{20,16},{24,28},{28,24},{1,5},{5... | collective-permute-start | bytes 1572872 | tf_op jit(solution)/shard_map/ppermute | solution.py:35
  9.0 33.6 %collective-permute-start.4 = (bf16[128,2176]{1,0:T(8,128)(2,1)}, bf16[128,2176]{1,0:T(8,128)(2,1)}, u32[]{:S(2)}, u32[]{:S(2)}) collective-permute-start(bf16[128,2176]{1,0:T(8,128)(2,1)} %pad_maximum_fusion.7), channel_id=1, source_target_pairs={{0,8},{4,12},{8,16},{12,20},{16,24},{20,28},{24,0},{28,4},{1,9},{5... | collective-permute-start | bytes 1671176 | tf_op jit(solution)/shard_map/ppermute | solution.py:32
  10.6 32.0 %collective-permute-start.5 = (bf16[128,2176]{1,0:T(8,128)(2,1)}, bf16[128,2176]{1,0:T(8,128)(2,1)}, u32[]{:S(2)}, u32[]{:S(2)}) collective-permute-start(bf16[128,2176]{1,0:T(8,128)(2,1)} %pad_maximum_fusion.7), channel_id=1, source_target_pairs={{0,4},{4,0},{8,12},{12,8},{16,20},{20,16},{24,28},{28,24},{1,5},{5... | collective-permute-start | bytes 1671176 | tf_op jit(solution)/shard_map/ppermute | solution.py:35
  16.5 3.4 %copy-start.8 = (bf16[128,2048]{1,0:T(8,128)(2,1)S(1)}, bf16[128,2048]{1,0:T(8,128)(2,1)}, u32[]{:S(2)}) copy-start(bf16[128,2048]{1,0:T(8,128)(2,1)} %param.7) | copy-start | bytes 1572868
  17.3 2.7 %copy-start.1 = (bf16[2048,1536]{1,0:T(8,128)(2,1)}, bf16[2048,1536]{1,0:T(8,128)(2,1)S(1)}, u32[]{:S(2)}) copy-start(bf16[2048,1536]{1,0:T(8,128)(2,1)S(1)} %pad_maximum_fusion) | copy-start | bytes 18874372
  25.3 0.7 copy-start.15
  25.3 0.7 copy-start.16
  26.2 9.2 %copy-start.20 = (bf16[1024,2048]{1,0:T(8,128)(2,1)S(1)}, bf16[1024,2048]{1,0:T(8,128)(2,1)}, u32[]{:S(2)}) copy-start(bf16[1024,2048]{1,0:T(8,128)(2,1)} %constant_dynamic-update-slice_fusion.13) | copy-start | bytes 12582916
  26.2 10.4 %copy-start.10 = (bf16[128,2048]{1,0:T(8,128)(2,1)S(1)}, bf16[128,2048]{1,0:T(8,128)(2,1)}, u32[]{:S(2)}) copy-start(bf16[128,2048]{1,0:T(8,128)(2,1)} %param.8) | copy-start | bytes 1572868
  32.3 5.4 %copy-start.19 = (bf16[128,768]{1,0:T(8,128)(2,1)S(1)}, bf16[128,768]{1,0:T(8,128)(2,1)}, u32[]{:S(2)}) copy-start(bf16[128,768]{1,0:T(8,128)(2,1)} %get-tuple-element.65) | copy-start | bytes 589828
  32.3 22.0 %collective-permute-start.2 = (bf16[128,2048]{1,0:T(8,128)(2,1)}, bf16[128,2048]{1,0:T(8,128)(2,1)S(1)}, u32[]{:S(2)}, u32[]{:S(2)}) collective-permute-start(bf16[128,2048]{1,0:T(8,128)(2,1)} %collective-permute-done), channel_id=1, source_target_pairs={{0,8},{4,12},{8,16},{12,20},{16,24},{20,28},{24,0},{28,4},{1,9},{5... | collective-permute-start | bytes 1572872 | tf_op jit(solution)/shard_map/ppermute | solution.py:32
  33.9 20.4 %collective-permute-start.3 = (bf16[128,2048]{1,0:T(8,128)(2,1)}, bf16[128,2048]{1,0:T(8,128)(2,1)S(1)}, u32[]{:S(2)}, u32[]{:S(2)}) collective-permute-start(bf16[128,2048]{1,0:T(8,128)(2,1)} %collective-permute-done), channel_id=1, source_target_pairs={{0,4},{4,0},{8,12},{12,8},{16,20},{20,16},{24,28},{28,24},{1,5},{5... | collective-permute-start | bytes 1572872 | tf_op jit(solution)/shard_map/ppermute | solution.py:35
  45.1 17.6 %collective-permute-start.8 = (bf16[128,2176]{1,0:T(8,128)(2,1)}, bf16[128,2176]{1,0:T(8,128)(2,1)S(1)}, u32[]{:S(2)}, u32[]{:S(2)}) collective-permute-start(bf16[128,2176]{1,0:T(8,128)(2,1)} %collective-permute-done.4), channel_id=1, source_target_pairs={{0,8},{4,12},{8,16},{12,20},{16,24},{20,28},{24,0},{28,4},{1,9},{5... | collective-permute-start | bytes 1671176 | tf_op jit(solution)/shard_map/ppermute | solution.py:32
  45.3 17.9 %collective-permute-start.9 = (bf16[128,2176]{1,0:T(8,128)(2,1)}, bf16[128,2176]{1,0:T(8,128)(2,1)S(1)}, u32[]{:S(2)}, u32[]{:S(2)}) collective-permute-start(bf16[128,2176]{1,0:T(8,128)(2,1)} %collective-permute-done.4), channel_id=1, source_target_pairs={{0,4},{4,0},{8,12},{12,8},{16,20},{20,16},{24,28},{28,24},{1,5},{5... | collective-permute-start | bytes 1671176 | tf_op jit(solution)/shard_map/ppermute | solution.py:35
  46.0 69.1 %collective-permute-start.13 = (bf16[128,2176]{1,0:T(8,128)(2,1)}, bf16[128,2176]{1,0:T(8,128)(2,1)S(1)}, u32[]{:S(2)}, u32[]{:S(2)}) collective-permute-start(bf16[128,2176]{1,0:T(8,128)(2,1)} %collective-permute-done.5), channel_id=1, source_target_pairs={{0,24},{4,28},{8,0},{12,4},{16,8},{20,12},{24,16},{28,20},{1,25},{... | collective-permute-start | bytes 1671176 | tf_op jit(solution)/shard_map/ppermute | solution.py:32
  49.5 2.2 slice-start
  49.7 2.7 %slice-start.1 = ((s8[6291456]{0:T(1024)(128)(4,1)}), s8[2097152]{0:T(1024)(128)(4,1)S(1)}, s32[]{:S(2)}) async-start(s8[6291456]{0:T(1024)(128)(4,1)} %bitcast.67), calls=%async_computation.1 | async-start | bytes 4194304
  54.2 2.0 copy-start.11
  54.3 31.6 %collective-permute-start.6 = (bf16[128,2048]{1,0:T(8,128)(2,1)S(1)}, bf16[128,2048]{1,0:T(8,128)(2,1)S(1)}, u32[]{:S(2)}, u32[]{:S(2)}) collective-permute-start(bf16[128,2048]{1,0:T(8,128)(2,1)S(1)} %collective-permute-done.2), channel_id=1, source_target_pairs={{0,8},{4,12},{8,16},{12,20},{16,24},{20,28},{24,0},{28,4},{1,9},{5... | collective-permute-start | bytes 1572872 | tf_op jit(solution)/shard_map/ppermute | solution.py:32
  54.3 32.1 %collective-permute-start.7 = (bf16[128,2048]{1,0:T(8,128)(2,1)S(1)}, bf16[128,2048]{1,0:T(8,128)(2,1)S(1)}, u32[]{:S(2)}, u32[]{:S(2)}) collective-permute-start(bf16[128,2048]{1,0:T(8,128)(2,1)S(1)} %collective-permute-done.2), channel_id=1, source_target_pairs={{0,4},{4,0},{8,12},{12,8},{16,20},{20,16},{24,28},{28,24},{1,5},{5... | collective-permute-start | bytes 1572872 | tf_op jit(solution)/shard_map/ppermute | solution.py:35
  62.7 110.4 %collective-permute-start.20 = (bf16[128,2048]{1,0:T(8,128)(2,1)}, bf16[128,2048]{1,0:T(8,128)(2,1)}, u32[]{:S(2)}, u32[]{:S(2)}) collective-permute-start(bf16[128,2048]{1,0:T(8,128)(2,1)} %slice.124), channel_id=1, source_target_pairs={{0,4},{4,0},{8,12},{12,8},{16,20},{20,16},{24,28},{28,24},{1,5},{5... | collective-permute-start | bytes 1572872 | tf_op jit(solution)/shard_map/ppermute | solution.py:35
  64.0 31.0 %collective-permute-start.11 = (bf16[128,2176]{1,0:T(8,128)(2,1)S(1)}, bf16[128,2176]{1,0:T(8,128)(2,1)S(1)}, u32[]{:S(2)}, u32[]{:S(2)}) collective-permute-start(bf16[128,2176]{1,0:T(8,128)(2,1)S(1)} %collective-permute-done.8), channel_id=1, source_target_pairs={{0,8},{4,12},{8,16},{12,20},{16,24},{20,28},{24,0},{28,4},{1,9},{5... | collective-permute-start | bytes 1671176 | tf_op jit(solution)/shard_map/ppermute | solution.py:32
  76.7 11.5 %copy-start.13 = (bf16[256,2048]{1,0:T(8,128)(2,1)}, bf16[256,2048]{1,0:T(8,128)(2,1)S(1)}, u32[]{:S(2)}) copy-start(bf16[256,2048]{1,0:T(8,128)(2,1)S(1)} %convolution_convert_fusion.3) | copy-start | bytes 3145732
  85.9 15.6 %collective-permute-start.12 = (bf16[128,2176]{1,0:T(8,128)(2,1)S(1)}, bf16[128,2176]{1,0:T(8,128)(2,1)S(1)}, u32[]{:S(2)}, u32[]{:S(2)}) collective-permute-start(bf16[128,2176]{1,0:T(8,128)(2,1)S(1)} %collective-permute-done.8), channel_id=1, source_target_pairs={{0,4},{4,0},{8,12},{12,8},{16,20},{20,16},{24,28},{28,24},{1,5},{5... | collective-permute-start | bytes 1671176 | tf_op jit(solution)/shard_map/ppermute | solution.py:35
  86.4 26.3 %collective-permute-start.10 = (bf16[128,2048]{1,0:T(8,128)(2,1)S(1)}, bf16[128,2048]{1,0:T(8,128)(2,1)S(1)}, u32[]{:S(2)}, u32[]{:S(2)}) collective-permute-start(bf16[128,2048]{1,0:T(8,128)(2,1)S(1)} %collective-permute-done.6), channel_id=1, source_target_pairs={{0,4},{4,0},{8,12},{12,8},{16,20},{20,16},{24,28},{28,24},{1,5},{5... | collective-permute-start | bytes 1572872 | tf_op jit(solution)/shard_map/ppermute | solution.py:35
  88.2 2.8 %copy-start.21 = (bf16[1024,2048]{1,0:T(8,128)(2,1)}, bf16[1024,2048]{1,0:T(8,128)(2,1)S(1)}, u32[]{:S(2)}) copy-start(bf16[1024,2048]{1,0:T(8,128)(2,1)S(1)} %constant_dynamic-update-slice_fusion.23) | copy-start | bytes 12582916
  88.2 2.8 %copy-start.22 = (bf16[1024,768]{1,0:T(8,128)(2,1)}, bf16[1024,768]{1,0:T(8,128)(2,1)S(1)}, u32[]{:S(2)}) copy-start(bf16[1024,768]{1,0:T(8,128)(2,1)S(1)} %constant_dynamic-update-slice_fusion.19) | copy-start | bytes 4718596
  95.0 55.8 %collective-permute-start.18 = (bf16[128,2048]{1,0:T(8,128)(2,1)}, bf16[128,2048]{1,0:T(8,128)(2,1)}, u32[]{:S(2)}, u32[]{:S(2)}) collective-permute-start(bf16[128,2048]{1,0:T(8,128)(2,1)} %slice.123), channel_id=1, source_target_pairs={{0,4},{4,0},{8,12},{12,8},{16,20},{20,16},{24,28},{28,24},{1,5},{5... | collective-permute-start | bytes 1572872 | tf_op jit(solution)/shard_map/ppermute | solution.py:35
  106.4 8.7 %copy-start.14 = (bf16[256,2048]{1,0:T(8,128)(2,1)}, bf16[256,2048]{1,0:T(8,128)(2,1)S(1)}, u32[]{:S(2)}) copy-start(bf16[256,2048]{1,0:T(8,128)(2,1)S(1)} %convolution_convert_fusion.2) | copy-start | bytes 3145732
  113.5 46.5 %collective-permute-start.16 = (bf16[128,2048]{1,0:T(8,128)(2,1)}, bf16[128,2048]{1,0:T(8,128)(2,1)}, u32[]{:S(2)}, u32[]{:S(2)}) collective-permute-start(bf16[128,2048]{1,0:T(8,128)(2,1)} %slice.121), channel_id=1, source_target_pairs={{0,4},{4,0},{8,12},{12,8},{16,20},{20,16},{24,28},{28,24},{1,5},{5... | collective-permute-start | bytes 1572872 | tf_op jit(solution)/shard_map/ppermute | solution.py:35
  115.1 2.1 copy-start.9
  115.1 2.0 copy-start.17
  120.1 42.6 %collective-permute-start.14 = (bf16[128,2048]{1,0:T(8,128)(2,1)}, bf16[128,2048]{1,0:T(8,128)(2,1)}, u32[]{:S(2)}, u32[]{:S(2)}) collective-permute-start(bf16[128,2048]{1,0:T(8,128)(2,1)} %convolution_convert_fusion.5), channel_id=1, source_target_pairs={{0,4},{4,0},{8,12},{12,8},{16,20},{20,16},{24,28},{28,24},{1,5},{5... | collective-permute-start | bytes 1572872 | tf_op jit(solution)/shard_map/ppermute | solution.py:35
  137.2 6.2 %copy-start.18 = (bf16[128,2176]{1,0:T(8,128)(2,1)S(1)}, bf16[128,2176]{1,0:T(8,128)(2,1)}, u32[]{:S(2)}) copy-start(bf16[128,2176]{1,0:T(8,128)(2,1)} %copy-done.17) | copy-start | bytes 1671172
  137.2 27.7 %collective-permute-start.21 = (bf16[2,512,1536]{1,2,0:T(8,128)(2,1)}, bf16[2,512,1536]{1,2,0:T(8,128)(2,1)}, u32[]{:S(2)}, u32[]{:S(2)}) collective-permute-start(bf16[2,512,1536]{1,2,0:T(8,128)(2,1)} %bitcast.73), channel_id=1, source_target_pairs={{0,1},{1,0},{2,3},{3,2},{4,5},{5,4},{6,7},{7,6},{8,9},{9,8},{10,11... | collective-permute-start | bytes 9437192 | tf_op jit(solution)/shard_map/ppermute | solution.py:38
  140.9 3.3 %copy-start.23 = (bf16[1024,768]{1,0:T(8,128)(2,1)S(1)}, bf16[1024,768]{1,0:T(8,128)(2,1)}, u32[]{:S(2)}) copy-start(bf16[1024,768]{1,0:T(8,128)(2,1)} %fusion.37) | copy-start | bytes 4718596
  150.1 0.7 copy-start.24
  150.1 0.7 copy-start.25
  150.1 0.7 copy-start.26
  150.1 1.2 copy-start.12
  150.6 3.1 %copy-start.2 = (bf16[2,4,96,2048]{3,2,0,1:T(8,128)(2,1)}, bf16[2,4,96,2048]{3,2,0,1:T(8,128)(2,1)S(1)}, u32[]{:S(2)}) copy-start(bf16[2,4,96,2048]{3,2,0,1:T(8,128)(2,1)S(1)} %copy.28) | copy-start | bytes 9437188
  150.8 8.8 %collective-permute-start.25 = (f32[1,128]{1,0:T(1,128)S(1)}, f32[1,128]{1,0:T(1,128)S(1)}, u32[]{:S(2)}, u32[]{:S(2)}) collective-permute-start(f32[1,128]{1,0:T(1,128)S(1)} %add_bitcast_fusion), channel_id=1, source_target_pairs={{0,1},{1,0},{2,3},{3,2},{4,5},{5,4},{6,7},{7,6},{8,9},{9,8},{10,11... | collective-permute-start | bytes 1544 | tf_op jit(solution)/shard_map/ppermute | solution.py:38
  159.6 6.5 %copy-start.6 = (bf16[2,1,512,1536]{2,3,0,1:T(8,128)(2,1)S(1)}, bf16[2,1,512,1536]{2,3,0,1:T(8,128)(2,1)}, u32[]{:S(2)}) copy-start(bf16[2,1,512,1536]{2,3,0,1:T(8,128)(2,1)} %copy.32) | copy-start | bytes 9437188
  159.6 49.3 %collective-permute-start.19 = (bf16[128,2048]{1,0:T(8,128)(2,1)}, bf16[128,2048]{1,0:T(8,128)(2,1)}, u32[]{:S(2)}, u32[]{:S(2)}) collective-permute-start(bf16[128,2048]{1,0:T(8,128)(2,1)} %add_convert_fusion.1), channel_id=1, source_target_pairs={{0,24},{4,28},{8,0},{12,4},{16,8},{20,12},{24,16},{28,20},{1,25},{... | collective-permute-start | bytes 1572872 | tf_op jit(solution)/shard_map/ppermute | solution.py:32
  160.1 10.1 %collective-permute-start.23 = (bf16[2,2,96,2048]{3,2,1,0:T(8,128)(2,1)}, bf16[2,2,96,2048]{3,2,1,0:T(8,128)(2,1)S(1)}, u32[]{:S(2)}, u32[]{:S(2)}) collective-permute-start(bf16[2,2,96,2048]{3,2,1,0:T(8,128)(2,1)} %dynamic-slice_bitcast_fusion), channel_id=1, source_target_pairs={{0,1},{1,0},{2,3},{3,2},{4,5},{5,4},{6,7},{7,6},{8,9},{9,8},{10,11... | collective-permute-start | bytes 4718600 | tf_op jit(solution)/shard_map/ppermute | solution.py:38
  162.7 46.2 %collective-permute-start.17 = (bf16[128,2048]{1,0:T(8,128)(2,1)}, bf16[128,2048]{1,0:T(8,128)(2,1)}, u32[]{:S(2)}, u32[]{:S(2)}) collective-permute-start(bf16[128,2048]{1,0:T(8,128)(2,1)} %add_convert_fusion.2), channel_id=1, source_target_pairs={{0,16},{4,20},{8,24},{12,28},{16,0},{20,4},{24,8},{28,12},{1,17},{... | collective-permute-start | bytes 1572872 | tf_op jit(solution)/shard_map/ppermute | solution.py:32
  164.8 44.1 %collective-permute-start.15 = (bf16[128,2048]{1,0:T(8,128)(2,1)}, bf16[128,2048]{1,0:T(8,128)(2,1)}, u32[]{:S(2)}, u32[]{:S(2)}) collective-permute-start(bf16[128,2048]{1,0:T(8,128)(2,1)} %add_convert_fusion.3), channel_id=1, source_target_pairs={{0,8},{4,12},{8,16},{12,20},{16,24},{20,28},{24,0},{28,4},{1,9},{5... | collective-permute-start | bytes 1572872 | tf_op jit(solution)/shard_map/ppermute | solution.py:32
  168.9 4.2 %copy-start.4 = (bf16[2,512,1536]{1,2,0:T(8,128)(2,1)}, bf16[2,512,1536]{1,2,0:T(8,128)(2,1)S(1)}, u32[]{:S(2)}) copy-start(bf16[2,512,1536]{1,2,0:T(8,128)(2,1)S(1)} %fusion) | copy-start | bytes 9437188
  168.9 3.6 %copy-start.3 = (bf16[2,4,96,2048]{3,2,0,1:T(8,128)(2,1)S(1)}, bf16[2,4,96,2048]{3,2,0,1:T(8,128)(2,1)}, u32[]{:S(2)}) copy-start(bf16[2,4,96,2048]{3,2,0,1:T(8,128)(2,1)} %copy-done.2) | copy-start | bytes 9437188
  170.2 58.2 %collective-permute-start.22 = (bf16[1,512,1536]{1,2,0:T(8,128)(2,1)}, bf16[1,512,1536]{1,2,0:T(8,128)(2,1)}, u32[]{:S(2)}, u32[]{:S(2)}) collective-permute-start(bf16[1,512,1536]{1,2,0:T(8,128)(2,1)} %constant_dynamic-slice_fusion.1), channel_id=1, source_target_pairs={{0,2},{1,3},{2,0},{3,1},{4,6},{5,7},{6,4},{7,5},{8,10},{9,11},{10,... | collective-permute-start | bytes 4718600 | tf_op jit(solution)/shard_map/ppermute | solution.py:38
  173.1 1.6 copy-start.7
  173.1 33.7 %collective-permute-start.26 = (f32[1,128]{1,0:T(1,128)S(1)}, f32[1,128]{1,0:T(1,128)S(1)}, u32[]{:S(2)}, u32[]{:S(2)}) collective-permute-start(f32[1,128]{1,0:T(1,128)S(1)} %add.191), channel_id=1, source_target_pairs={{0,2},{1,3},{2,0},{3,1},{4,6},{5,7},{6,4},{7,5},{8,10},{9,11},{10,... | collective-permute-start | bytes 1544 | tf_op jit(solution)/shard_map/ppermute | solution.py:38
  206.9 19.0 %collective-permute-start.24 = (bf16[1,2,96,2048]{3,2,1,0:T(8,128)(2,1)}, bf16[1,2,96,2048]{3,2,1,0:T(8,128)(2,1)}, u32[]{:S(2)}, u32[]{:S(2)}) collective-permute-start(bf16[1,2,96,2048]{3,2,1,0:T(8,128)(2,1)} %constant_dynamic-slice_fusion), channel_id=1, source_target_pairs={{0,2},{1,3},{2,0},{3,1},{4,6},{5,7},{6,4},{7,5},{8,10},{9,11},{10,... | collective-permute-start | bytes 2359304 | tf_op jit(solution)/shard_map/ppermute | solution.py:38
  208.4 20.0 %copy-start.5 = (bf16[2,512,1536]{1,2,0:T(8,128)(2,1)S(1)}, bf16[2,512,1536]{1,2,0:T(8,128)(2,1)}, u32[]{:S(2)}) copy-start(bf16[2,512,1536]{1,2,0:T(8,128)(2,1)} %copy-done.4) | copy-start | bytes 9437188

commit v2 on v1

v2 whole, which is shorter than its diff:
```python
import jax
import jax.numpy as jnp
from jax import lax
from jax.sharding import PartitionSpec as P

BF = jnp.bfloat16
F32 = jnp.float32
LANES = 128


def dot(a, b, ca, cb):
    return lax.dot_general(a, b, (((ca,), (cb,)), ((), ())), preferred_element_type=F32)


def tie(*values):
    return lax.optimization_barrier(values)


def shards(tokens, out_grad, route_weights, expert_ids, gate_weight, up_weight, down_weight):
    local_experts, width, hidden = gate_weight.shape
    devices = lax.axis_size("expert")
    groups = lax.axis_size("dp")
    num_experts = local_experts * devices
    rows, top_count = expert_ids.shape
    outer = devices // 2
    inner_width = local_experts * hidden
    me = lax.axis_index("expert")
    my_group = lax.axis_index("dp")

    def ring(value, step):
        pairs = [(2 * z + x, 2 * ((z + step) % outer) + x) for z in range(outer) for x in range(2)]
        return lax.ppermute(value, "expert", pairs)

    def cross(value):
        return lax.ppermute(value, "expert", [(i, i ^ 1) for i in range(devices)])

    def swap(value, bit):
        return lax.ppermute(value, "dp", [(i, i ^ bit) for i in range(groups)])

    lanes = jnp.arange(LANES, dtype=jnp.int32)
    dense = jnp.sum(
        jnp.where(
            expert_ids[:, :, None] == lanes, route_weights.astype(F32)[:, :, None], 0.0
        ),
        axis=1,
    ).astype(BF)
    grads = jnp.concatenate([out_grad, dense], axis=1)

    gate_up = jnp.concatenate(
        [gate_weight[e] for e in range(local_experts)] + [up_weight[e] for e in range(local_experts)],
        axis=1,
    )
    down = down_weight.reshape(inner_width, width)

    def middle(linear, grad_rows):
        cotangent = grad_rows[:, :width]
        routes = grad_rows[:, width:].astype(F32)
        weight = jnp.concatenate(
            [
                jnp.broadcast_to(
                    jnp.sum(
                        jnp.where(lanes == me * local_experts + e, routes, 0.0), axis=1, keepdims=True
                    ),
                    (grad_rows.shape[0], hidden),
                )
                for e in range(local_experts)
            ],
            axis=1,
        )
        gate_linear = linear[:, :inner_width]
        up_linear = linear[:, inner_width:]
        delta_hidden = weight * dot(cotangent, down, 1, 1)
        logistic = jax.nn.sigmoid(gate_linear)
        activated = gate_linear * logistic
        scaled_hidden = (weight * activated * up_linear).astype(BF)
        delta_gate = delta_hidden * up_linear * logistic * (1.0 + gate_linear * (1.0 - logistic))
        delta_up = delta_hidden * activated
        delta = jnp.concatenate([delta_gate.astype(BF), delta_up.astype(BF)], axis=1)
        return delta, scaled_hidden

    def partial_input(delta):
        return dot(delta, gate_up, 1, 1).astype(BF)

    flying_a = (ring(tokens, 1), cross(tokens))
    flying_b = (ring(grads, 1), cross(grads))
    gate_up = tie(gate_up, grads)[0]
    token_blocks, grad_blocks, deltas, hiddens, partials = [], [], [], [], []
    first_grad_cross = None
    for step in range(1, outer):
        got = tie(*flying_a, *((deltas[-1], hiddens[-1], partials[-1]) if partials else ()))
        if partials:
            deltas[-1], hiddens[-1], partials[-1] = got[2:]
        flying_a = (cross(got[0]),) if step == outer - 1 else (ring(got[0], 1), cross(got[0]))
        here = ((tokens,) if step == 1 else ()) + tuple(got[:2])
        token_blocks.append(jnp.concatenate(here, axis=0))
        linear = dot(token_blocks[-1], gate_up, 1, 0)
        got = tie(*flying_b, linear)
        if step == 1:
            first_grad_cross = got[1]
        flying_b = (ring(first_grad_cross, outer - 1),) if step == outer - 1 else (ring(got[0], 1), cross(got[0]))
        here = ((grads,) if step == 1 else ()) + tuple(got[:2])
        grad_blocks.append(jnp.concatenate(here, axis=0))
        delta, scaled_hidden = middle(got[2], grad_blocks[-1])
        deltas.append(delta)
        hiddens.append(scaled_hidden)
        partials.append(partial_input(delta))

    def stacked(blocks):
        return jnp.concatenate(blocks, axis=0) if len(blocks) > 1 else blocks[0]

    def cotangents(blocks):
        return stacked([g[:, :width] for g in blocks])

    early_gate_up = dot(stacked(token_blocks[:-1]), stacked(deltas[:-1]), 0, 0).astype(BF)
    early_down = dot(stacked(hiddens[:-1]), cotangents(grad_blocks[:-1]), 0, 0).astype(BF)

    (last_tokens,) = flying_a
    last_tokens, early_gate_up, early_down = tie(last_tokens, early_gate_up, early_down)
    linear = dot(last_tokens, gate_up, 1, 0)
    got = tie(*flying_b, linear, deltas[-1], hiddens[-1], *partials)
    last_grads, linear, deltas[-1], hiddens[-1] = got[:4]
    partials = list(got[4:])
    own = [partials[0][:rows], partials[0][rows : 2 * rows]] + [p[:rows] for p in partials[1:]]
    other = [p[-rows:] for p in partials]

    order = list(range(outer - 2, 0, -1))
    crossed = {s: cross(other[s]) for s in order}
    token_blocks.append(last_tokens)
    grad_blocks.append(last_grads)
    load = sum(jnp.sum(g[:, width:].astype(F32), axis=0, keepdims=True) for g in grad_blocks)
    flying_load = swap(load, 1)
    delta, scaled_hidden = middle(linear, last_grads)
    deltas.append(delta)
    hiddens.append(scaled_hidden)

    late_tokens = stacked(token_blocks[-2:])
    late_grads = cotangents(grad_blocks[-2:])
    late_delta = stacked(deltas[-2:])
    late_hidden = stacked(hiddens[-2:])
    near, far = my_group, my_group ^ 2
    part = width // groups

    def gate_up_chunk(index, late_delta):
        columns = lax.dynamic_slice(late_tokens, (0, index * part), (late_tokens.shape[0], part))
        before = lax.dynamic_slice(early_gate_up, (index * part, 0), (part, early_gate_up.shape[1]))
        return (dot(columns, late_delta, 0, 0) + before.astype(F32)).astype(BF)

    def down_chunk(index):
        return lax.dynamic_index_in_dim(all_down, index, 1, keepdims=False)

    def add(a, b):
        return (a.astype(F32) + b.astype(F32)).astype(BF)

    all_down = (dot(late_hidden, late_grads, 0, 0) + early_down.astype(F32)).astype(BF)
    all_down, late_delta = tie(all_down, late_delta)
    all_down = all_down.reshape(local_experts, groups, hidden // groups, width)
    flying_down = swap(down_chunk(far ^ 1), 1)
    far_other = gate_up_chunk(far ^ 1, late_delta)
    flying_down, flying_load, far_other, late_delta, delta = tie(flying_down, flying_load, far_other, late_delta, delta)
    load = load + flying_load
    flying_load = swap(load, 2)
    flying_gate_up = swap(far_other, 1)
    far_down_sum = add(down_chunk(far), flying_down)
    flying_down = swap(far_down_sum, 2)
    far_mine = gate_up_chunk(far, late_delta)
    flying_gate_up, far_mine, delta, late_delta = tie(flying_gate_up, far_mine, delta, late_delta)
    far_sum = add(far_mine, flying_gate_up)
    flying_gate_up = swap(far_sum, 2)
    last_partial = partial_input(delta)
    near_other = gate_up_chunk(near ^ 1, late_delta)
    got = tie(far_sum, last_partial, near_other, late_delta, partials[0], *(crossed[s] for s in order))
    far_sum, last_partial, near_other, late_delta, first_partial = got[:5]
    crossed_last = cross(last_partial)
    near_gate_up = swap(near_other, 1)
    near_down = swap(down_chunk(near ^ 1), 1)
    back = []
    for s, value in zip(order, got[5:]):
        back.append(ring(add(own[s], value), outer - s))
    crossed_first = cross(first_partial[-rows:])
    near_mine = gate_up_chunk(near, late_delta)
    near_gate_up, near_down, near_mine, crossed_last = tie(near_gate_up, near_down, near_mine, crossed_last)
    back.append(ring(add(own[-1], crossed_last), 1))
    near_down = add(down_chunk(near), near_down)
    near_gate_up = add(near_mine, near_gate_up)
    got = tie(crossed_first, near_down, near_gate_up, *back)
    crossed_first, near_down, near_gate_up = got[:3]
    total = own[0].astype(F32) + crossed_first.astype(F32)
    for value in got[3:]:
        total = total + value.astype(F32)
    grad_input = total.astype(BF)
    flying_down, flying_load, grad_input, near_down = tie(flying_down, flying_load, grad_input, near_down)
    load = load + flying_load
    expert_load = load[0, :num_experts] * (num_experts / (rows * devices * groups * top_count))

    factor = 1.0 / groups
    out_down = ((near_down.astype(F32) + flying_down.astype(F32)) * factor).astype(BF)
    flying_gate_up, near_gate_up, out_down = tie(flying_gate_up, near_gate_up, out_down)
    out_gate, out_up = [], []
    for kind, out in ((0, out_gate), (1, out_up)):
        for e in range(local_experts):
            at = slice((kind * local_experts + e) * hidden, (kind * local_experts + e + 1) * hidden)
            value = near_gate_up[:, at].astype(F32) + flying_gate_up[:, at].astype(F32)
            out.append((value * factor).astype(BF))
    out_gate, out_up = jnp.stack(out_gate), jnp.stack(out_up)
    return (grad_input, out_gate, out_up, out_down, expert_load)


def solution(mesh):
    return jax.shard_map(
        shards,
        mesh=mesh,
        in_specs=(
            P(("expert", "dp"), None),
            P(("expert", "dp"), None),
            P(("expert", "dp"), None),
            P(("expert", "dp"), None),
            P("expert", None, None),
            P("expert", None, None),
            P("expert", None, None),
        ),
        out_specs=(
            P(("expert", "dp"), None),
            P("expert", "dp", None),
            P("expert", "dp", None),
            P("expert", "dp", None),
            P(),
        ),
        check_vma=False,
    )
```

time: 237 us -> 193 us (0.81)
  local copies, waits for them, and re-layouts: 50.5 us -> 17 us
  waiting for transfers between devices: 72.9 us -> 57.2 us
  starting transfers between devices: 37.2 us -> 40.5 us
  other arithmetic: 25.5 us -> 23 us
    ppermute x6 -> x8, waiting for transfers between devices: 45 us -> 1.83 us  [swap(): return lax.ppermute(value, 'dp', [(i, i ^ bit) for i in range(groups)])]
    unnamed x84 -> x45, local copies, waits for them, and re-layouts: 26.1 us -> 5.89 us
    ppermute x10, waiting for transfers between devices: 17 us -> 34 us  [ring(): return lax.ppermute(value, 'expert', pairs)]
    ppermute x11, waiting for transfers between devices: 10.9 us -> 21.4 us  [cross(): return lax.ppermute(value, 'expert', [(i, i ^ 1) for i in range(devices)])]
    dynamic_slice x2 -> x0, local copies, waits for them, and re-layouts: 7.8 us -> none  [the longest x1 4.71 us: reduce_groups(): theirs = lax.dynamic_index_in_dim(value, 1 - low, 1, keepdims=False)]
    convert_element_type x7, other arithmetic: 14.6 us -> 10.4 us  [the longest x6 9.27 us: add(): return (a.astype(F32) + b.astype(F32)).astype(BF)]
    ppermute x10, starting transfers between devices: 21 us -> 23.8 us  [ring(): return lax.ppermute(value, 'expert', pairs)]
    concatenate x1, other arithmetic: 0.73 us -> 3.16 us  [shards(): jnp.concatenate([gate_weight[e] for e in range(local_experts)] + [up_weig...]
  transfers between devices with their start and end apart: 27 -> 29, of which waited for: 7 -> 10; matrix products, arithmetic and copies ran while one was open for 47% -> 42% of each run, Pallas kernels for 0% -> 0%
where the time goes in v2:
time: 193 us; the launch traced here: 190 us
  waiting for transfers between devices  57.2 us (30%)
  matrix products  50.8 us (26%)
  starting transfers between devices  40.5 us (21%)
  other arithmetic  23 us (12%)
  local copies, waits for them, and re-layouts  17 us (9%)
    dot_general x19, matrix products, dot(): lax.dot_general(a, b, (((ca,), (cb,)), ((), ())), preferred_element_type=...  50.8 us
    ppermute x10, waiting for transfers between devices, ring(): return lax.ppermute(value, 'expert', pairs)  34 us
    ppermute x10, starting transfers between devices, ring(): return lax.ppermute(value, 'expert', pairs)  23.8 us
    ppermute x11, waiting for transfers between devices, cross(): return lax.ppermute(value, 'expert', [(i, i ^ 1) for i in range(devices)])  21.4 us
    ppermute x11, starting transfers between devices, cross(): return lax.ppermute(value, 'expert', [(i, i ^ 1) for i in range(devices)])  12.9 us
    convert_element_type x6, other arithmetic, add(): return (a.astype(F32) + b.astype(F32)).astype(BF)  9.27 us
    unnamed x45, local copies, waits for them, and re-layouts  5.89 us
  transfers between devices with their start and end apart: 29, of which 10 were waited for; matrix products, arithmetic and copies ran while one was open for 42% of the time, Pallas kernels for 0%

profile of v2, /device:TPU:0, one launch (start us, length us, event | category | flops | bytes accessed | tf_op | source)
XLA Modules:
  0.0 189.7 jit_solution(2109294341094978489)
XLA Ops:
  0.6 3.1 %collective-permute-start.2 = (bf16[128,2048]{1,0:T(8,128)(2,1)}, bf16[128,2048]{1,0:T(8,128)(2,1)}, u32[]{:S(2)}, u32[]{:S(2)}) collective-permute-start(bf16[128,2048]{1,0:T(8,128)(2,1)} %param.7), channel_id=1, source_target_pairs={{0,8},{4,12},{8,16},{12,20},{16,24},{20,28},{24,0},{28,4},{1,9},{5... | collective-permute-start | bytes 1572872 | tf_op jit(solution)/shard_map/ppermute | solution.py:32
  3.7 1.5 collective-permute-start.3
  7.1 1.9 pad_maximum_fusion.12
  9.0 1.6 collective-permute-start
  11.2 3.5 %slice_bitcast_fusion.1 = (bf16[2048,384]{1,0:T(8,128)(2,1)S(1)}, bf16[2048,384]{1,0:T(8,128)(2,1)S(1)}, bf16[2048,384]{1,0:T(8,128)(2,1)S(1)}, bf16[2048,384]{1,0:T(8,128)(2,1)S(1)}) fusion(bf16[2,2048,384]{2,1,0:T(8,128)(2,1)} %param.12, bf16[2,2048,384]{2,1,0:T(8,128)(2,1)} %param.11), kind=kLoop, calls=%fused_computation.42 | loop fusion | bytes 12582912 | tf_op jit(solution)/shard_map/squeeze | solution.py:50
  14.6 3.2 %pad_maximum_fusion = bf16[2048,1536]{1,0:T(8,128)(2,1)} fusion(bf16[2048,384]{1,0:T(8,128)(2,1)S(1)} %get-tuple-element.162, bf16[2048,384]{1,0:T(8,128)(2,1)S(1)} %get-tuple-element.161, bf16[2048,384]{1,0:T(8,128)(2,1)S(1)} %get-tuple-element.173, bf16[2048,384]{1,0:T(8,128)(2,1)S(1)} %get-tuple-element.174), kind=kLoop, calls=%fused_computation.1 | loop fusion | flops 25165824 | bytes 12582912 | tf_op jit(solution)/shard_map/concatenate | solution.py:49
  17.8 1.2 constant_dynamic-update-slice_fusion.6
  19.0 1.6 collective-permute-start.5
  20.6 1.5 collective-permute-start.6
  22.1 1.1 constant_dynamic-update-slice_fusion.5
  23.2 1.1 constant_dynamic-update-slice_fusion.4
  24.3 5.0 %fusion.9 = f32[384,1536]{1,0:T(8,128)S(1)} fusion(bf16[2048,1536]{1,0:T(8,128)(2,1)} %pad_maximum_fusion, bf16[128,2048]{1,0:T(8,128)(2,1)} %collective-permute-done.3, bf16[128,2048]{1,0:T(8,128)(2,1)} %collective-permute-done.2, bf16[128,2048]{1,0:T(8,128)(2,1)S(1)} %copy-done.12), kind=kOutput, calls=%fused_computation.26 | convolution fusion | flops 2420637696 | bytes 10223616 | tf_op jit(solution)/shard_map/dot_general | solution.py:12
  29.4 1.4 collective-permute-done
  30.8 1.6 collective-permute-start.9
  32.4 1.5 collective-permute-start.10
  33.9 1.4 pad_maximum_fusion.1
  35.3 2.5 %collective-permute-start.4 = (bf16[128,2176]{1,0:T(8,128)(2,1)}, bf16[128,2176]{1,0:T(8,128)(2,1)S(1)}, u32[]{:S(2)}, u32[]{:S(2)}) collective-permute-start(bf16[128,2176]{1,0:T(8,128)(2,1)} %collective-permute-done.1), channel_id=1, source_target_pairs={{0,24},{4,28},{8,0},{12,4},{16,8},{20,12},{24,16},{28,20},{1,25},{... | collective-permute-start | bytes 1671176 | tf_op jit(solution)/shard_map/ppermute | solution.py:32
  39.0 2.0 %multiply_convert_fusion.2 = (bf16[384,768]{1,0:T(8,128)(2,1)S(1)}, bf16[384,768]{1,0:T(8,128)(2,1)S(1)}, bf16[384,768]{1,0:T(8,128)(2,1)S(1)}) fusion(f32[384,1536]{1,0:T(8,128)S(1)} %fusion.9, f32[384,384]{1,0:T(8,128)S(1)} %broadcast_in_dim.113, f32[384,384]{1,0:T(8,128)S(1)} %broadcast_in_dim.111, bf16[384,2048]{1,0:T(8,128)(2,1)S(1)} %pad_maximum_fusion.1, ...), kind=kOutput, calls=%fused_computation.56 | convolution fusion | flops 1213267968 | bytes 10027008 | tf_op jit(solution)/shard_map/dot_general | solution.py:12
  41.8 3.8 %convolution_convert_fusion.2 = bf16[384,2048]{1,0:T(8,128)(2,1)} fusion(bf16[2048,1536]{1,0:T(8,128)(2,1)S(1)} %bitcast.61, bf16[384,768]{1,0:T(8,128)(2,1)S(1)} %get-tuple-element.150, bf16[384,768]{1,0:T(8,128)(2,1)S(1)} %get-tuple-element.149), kind=kOutput, calls=%fused_computation.13 | convolution fusion | flops 2419064832 | bytes 9043968 | tf_op jit(solution)/shard_map/dot_general | solution.py:12
  46.1 1.8 fusion.27
  47.9 5.9 %collective-permute-done.9 = bf16[128,2176]{1,0:T(8,128)(2,1)S(1)} collective-permute-done((bf16[128,2176]{1,0:T(8,128)(2,1)}, bf16[128,2176]{1,0:T(8,128)(2,1)S(1)}, u32[]{:S(2)}, u32[]{:S(2)}) %collective-permute-start.9) | collective-permute-done | bytes 557088 | tf_op jit(solution)/shard_map/ppermute | solution.py:32
  54.2 10.9 %collective-permute-start.12 = (bf16[128,2176]{1,0:T(8,128)(2,1)S(1)}, bf16[128,2176]{1,0:T(8,128)(2,1)S(1)}, u32[]{:S(2)}, u32[]{:S(2)}) collective-permute-start(bf16[128,2176]{1,0:T(8,128)(2,1)S(1)} %collective-permute-done.9), channel_id=1, source_target_pairs={{0,8},{4,12},{8,16},{12,20},{16,24},{20,28},{24,0},{28,4},{1,9},{5... | collective-permute-start | bytes 1671176 | tf_op jit(solution)/shard_map/ppermute | solution.py:32
  65.2 1.5 collective-permute-start.13
  66.9 2.1 %multiply_convert_fusion.10 = (bf16[256,768]{1,0:T(8,128)(2,1)S(1)}, bf16[256,768]{1,0:T(8,128)(2,1)S(1)}, bf16[256,768]{1,0:T(8,128)(2,1)}) fusion(f32[256,1536]{1,0:T(8,128)S(1)} %fusion.27, f32[256,384]{1,0:T(8,128)S(1)} %broadcast_in_dim.118, f32[256,384]{1,0:T(8,128)S(1)} %broadcast_in_dim.116, bf16[768,2048]{1,0:T(8,128)(2,1)S(1)} %bitcast.57, ...), kind=kOutput, calls=%fused_computation.97 | convolution fusion | flops 808845312 | bytes 7733248 | tf_op jit(solution)/shard_map/dot_general | solution.py:12
  69.0 2.9 %convolution_convert_fusion.4 = bf16[256,2048]{1,0:T(8,128)(2,1)} fusion(bf16[2048,1536]{1,0:T(8,128)(2,1)S(1)} %bitcast.61, bf16[256,768]{1,0:T(8,128)(2,1)S(1)} %get-tuple-element.166, bf16[256,768]{1,0:T(8,128)(2,1)S(1)} %get-tuple-element.165), kind=kOutput, calls=%fused_computation.18 | convolution fusion | flops 1612709888 | bytes 8126464 | tf_op jit(solution)/shard_map/dot_general | solution.py:12
  71.9 5.1 %collective-permute-done.7 = bf16[128,2048]{1,0:T(8,128)(2,1)S(1)} collective-permute-done((bf16[128,2048]{1,0:T(8,128)(2,1)S(1)}, bf16[128,2048]{1,0:T(8,128)(2,1)S(1)}, u32[]{:S(2)}, u32[]{:S(2)}) %collective-permute-start.7) | collective-permute-done | bytes 524320 | tf_op jit(solution)/shard_map/ppermute | solution.py:32
  77.0 1.7 collective-permute-start.11
  78.8 5.4 %convolution_convert_fusion = bf16[2048,1536]{1,0:T(8,128)(2,1)S(1)} fusion(bf16[640,2048]{1,0:T(8,128)(2,1)S(1)} %constant_dynamic-update-slice_fusion.2, bf16[256,1536]{1,0:T(8,128)(2,1)S(1)} %pad_maximum_fusion.7, bf16[384,1536]{1,0:T(8,128)(2,1)S(1)} %pad_maximum_fusion.5), kind=kOutput, calls=%fused_computation | convolution fusion | flops 4033609728 | bytes 10878976 | tf_op jit(solution)/shard_map/dot_general | solution.py:12
  84.3 3.1 %convolution_convert_fusion.1 = bf16[768,2048]{1,0:T(8,128)(2,1)S(1)} fusion(bf16[256,2048]{1,0:T(8,128)(2,1)S(1)} %slice.153, bf16[384,2048]{1,0:T(8,128)(2,1)S(1)} %pad_maximum_fusion.1, bf16[256,768]{1,0:T(8,128)(2,1)S(1)} %copy-done.13, bf16[384,768]{1,0:T(8,128)(2,1)S(1)} %get-tuple-element.85), kind=kOutput, calls=%fused_computation.3 | convolution fusion | flops 2022047744 | bytes 6750208 | tf_op jit(solution)/shard_map/dot_general | solution.py:12
  87.5 1.8 fusion.31
  89.8 1.4 multiply_convert_fusion.8
  91.2 2.8 %convolution_convert_fusion.3 = bf16[256,2048]{1,0:T(8,128)(2,1)} fusion(bf16[2048,1536]{1,0:T(8,128)(2,1)S(1)} %bitcast.61, bf16[256,768]{1,0:T(8,128)(2,1)S(1)} %get-tuple-element.164, bf16[256,768]{1,0:T(8,128)(2,1)S(1)} %get-tuple-element.163), kind=kOutput, calls=%fused_computation.17 | convolution fusion | flops 1612709888 | bytes 8126464 | tf_op jit(solution)/shard_map/dot_general | solution.py:12
  94.2 1.0 fusion.85
  95.5 1.3 multiply_convert_fusion.12
  96.9 1.1 slice-done.4
  98.0 1.9 add_convert_fusion
  99.9 1.2 dynamic-slice_bitcast_fusion
  102.3 2.2 %add_convert_fusion.3 = bf16[512,1536]{1,0:T(8,128)(2,1)} fusion(bf16[2048,1536]{1,0:T(8,128)(2,1)S(1)} %convolution_convert_fusion, s32[]{:T(128)S(6)} %select_n.71, bf16[384,1536]{1,0:T(8,128)(2,1)S(1)} %maximum_maximum_fusion, bf16[384,2048]{1,0:T(8,128)(2,1)S(1)} %constant_dynamic-update-slice_fusion.9), kind=kOutput, calls=%fused_computation.9 | convolution fusion | flops 606339072 | bytes 4719616 | tf_op jit(solution)/shard_map/dot_general | solution.py:12
  104.7 1.2 slice.137
  106.3 1.1 slice.138
  107.4 1.8 collective-permute-start.20
  109.2 2.7 %fusion = bf16[512,1536]{1,0:T(8,128)(2,1)S(1)} fusion(bf16[384,1536]{1,0:T(8,128)(2,1)S(1)} %copy-done.2, bf16[2048,1536]{1,0:T(8,128)(2,1)} %copy-done.4, s32[]{:T(128)S(6)} %select_n.72, bf16[384,2048]{1,0:T(8,128)(2,1)} %copy-done.8), kind=kOutput, calls=%fused_computation.10 | convolution fusion | flops 606339072 | bytes 4719616 | tf_op jit(solution)/shard_map/dot_general | solution.py:12
  111.9 3.1 %add_convert_fusion.2 = bf16[512,1536]{1,0:T(8,128)(2,1)} fusion(bf16[512,1536]{1,0:T(8,128)(2,1)} %collective-permute-done.18, bf16[512,1536]{1,0:T(8,128)(2,1)S(1)} %fusion), kind=kLoop, calls=%fused_computation.8 | loop fusion | flops 3145728 | bytes 4718592 | tf_op jit(solution)/shard_map/convert_element_type | solution.py:152
  115.0 3.7 %fusion.1 = bf16[512,1536]{1,0:T(8,128)(2,1)} fusion(bf16[384,1536]{1,0:T(8,128)(2,1)S(1)} %copy-done.2, bf16[2048,1536]{1,0:T(8,128)(2,1)} %copy-done.4, s32[]{:T(128)S(6)} %select_n.73, bf16[384,2048]{1,0:T(8,128)(2,1)} %copy-done.8), kind=kOutput, calls=%fused_computation.11 | convolution fusion | flops 606339072 | bytes 4719616 | tf_op jit(solution)/shard_map/dot_general | solution.py:12
  118.7 3.2 %convolution_convert_fusion.5 = bf16[128,2048]{1,0:T(8,128)(2,1)} fusion(bf16[128,1536]{1,0:T(8,128)(2,1)S(1)} %pad_maximum_fusion.14, bf16[2048,1536]{1,0:T(8,128)(2,1)S(1)} %bitcast.63), kind=kOutput, calls=%fused_computation.19 | convolution fusion | flops 805568512 | bytes 7208960 | tf_op jit(solution)/shard_map/dot_general | solution.py:12
  121.9 9.7 %collective-permute-done.20 = bf16[128,2048]{1,0:T(8,128)(2,1)} collective-permute-done((bf16[128,2048]{1,0:T(8,128)(2,1)S(1)}, bf16[128,2048]{1,0:T(8,128)(2,1)}, u32[]{:S(2)}, u32[]{:S(2)}) %collective-permute-start.20) | collective-permute-done | bytes 524320 | tf_op jit(solution)/shard_map/ppermute | solution.py:35
  132.1 1.5 collective-permute-start.28
  134.2 1.1 slice.139
  135.3 1.6 collective-permute-start.21
  136.8 1.3 add_convert_fusion.7
  138.2 2.7 %fusion.2 = bf16[512,1536]{1,0:T(8,128)(2,1)S(1)} fusion(bf16[384,1536]{1,0:T(8,128)(2,1)S(1)} %copy-done.3, bf16[2048,1536]{1,0:T(8,128)(2,1)} %copy-done.4, s32[]{:T(128)S(6)} %select_n.76, bf16[384,2048]{1,0:T(8,128)(2,1)} %copy-done.8), kind=kOutput, calls=%fused_computation.12 | convolution fusion | flops 606339072 | bytes 4719616 | tf_op jit(solution)/shard_map/dot_general | solution.py:12
  140.9 1.2 add_convert_fusion.6
  142.9 5.8 %collective-permute-done.24 = bf16[128,2048]{1,0:T(8,128)(2,1)S(1)} collective-permute-done((bf16[128,2048]{1,0:T(8,128)(2,1)}, bf16[128,2048]{1,0:T(8,128)(2,1)S(1)}, u32[]{:S(2)}, u32[]{:S(2)}) %collective-permute-start.24) | collective-permute-done | bytes 524320 | tf_op jit(solution)/shard_map/ppermute | solution.py:35
  148.7 1.8 collective-permute-start.26
  150.5 1.8 fusion.21
  152.9 5.8 %collective-permute-done.21 = bf16[128,2048]{1,0:T(8,128)(2,1)S(1)} collective-permute-done((bf16[128,2048]{1,0:T(8,128)(2,1)S(1)}, bf16[128,2048]{1,0:T(8,128)(2,1)S(1)}, u32[]{:S(2)}, u32[]{:S(2)}) %collective-permute-start.21) | collective-permute-done | bytes 524320 | tf_op jit(solution)/shard_map/ppermute | solution.py:35
  158.7 1.8 add_convert_fusion.1
  160.5 8.0 %collective-permute-done.25 = bf16[128,2048]{1,0:T(8,128)(2,1)S(1)} collective-permute-done((bf16[128,2048]{1,0:T(8,128)(2,1)S(1)}, bf16[128,2048]{1,0:T(8,128)(2,1)S(1)}, u32[]{:S(2)}, u32[]{:S(2)}) %collective-permute-start.25) | collective-permute-done | bytes 524320 | tf_op jit(solution)/shard_map/ppermute | solution.py:32
  169.0 13.5 %collective-permute-done.26 = bf16[128,2048]{1,0:T(8,128)(2,1)S(1)} collective-permute-done((bf16[128,2048]{1,0:T(8,128)(2,1)S(1)}, bf16[128,2048]{1,0:T(8,128)(2,1)S(1)}, u32[]{:S(2)}, u32[]{:S(2)}) %collective-permute-start.26) | collective-permute-done | bytes 524320 | tf_op jit(solution)/shard_map/ppermute | solution.py:32
  182.6 1.2 add_convert_fusion.4
  183.8 1.8 collective-permute-done.17
  185.6 1.2 multiply_convert_fusion
  187.8 1.0 pad_maximum_fusion.10
  188.8 1.0 pad_maximum_fusion.11
  (111 shorter events, 12.7 us)
Async XLA Ops:
  0.6 38.3 %copy-start = (bf16[2,384,2048]{2,1,0:T(8,128)(2,1)S(1)}, bf16[2,384,2048]{2,1,0:T(8,128)(2,1)}, u32[]{:S(2)}) copy-start(bf16[2,384,2048]{2,1,0:T(8,128)(2,1)} %param.13) | copy-start | bytes 9437188
  0.6 18.3 %collective-permute-start.2 = (bf16[128,2048]{1,0:T(8,128)(2,1)}, bf16[128,2048]{1,0:T(8,128)(2,1)}, u32[]{:S(2)}, u32[]{:S(2)}) collective-permute-start(bf16[128,2048]{1,0:T(8,128)(2,1)} %param.7), channel_id=1, source_target_pairs={{0,8},{4,12},{8,16},{12,20},{16,24},{20,28},{24,0},{28,4},{1,9},{5... | collective-permute-start | bytes 1572872 | tf_op jit(solution)/shard_map/ppermute | solution.py:32
  3.7 15.2 %collective-permute-start.3 = (bf16[128,2048]{1,0:T(8,128)(2,1)}, bf16[128,2048]{1,0:T(8,128)(2,1)}, u32[]{:S(2)}, u32[]{:S(2)}) collective-permute-start(bf16[128,2048]{1,0:T(8,128)(2,1)} %param.7), channel_id=1, source_target_pairs={{0,4},{4,0},{8,12},{12,8},{16,20},{20,16},{24,28},{28,24},{1,5},{5... | collective-permute-start | bytes 1572872 | tf_op jit(solution)/shard_map/ppermute | solution.py:35
  9.0 21.7 %collective-permute-start = (bf16[128,2176]{1,0:T(8,128)(2,1)}, bf16[128,2176]{1,0:T(8,128)(2,1)}, u32[]{:S(2)}, u32[]{:S(2)}) collective-permute-start(bf16[128,2176]{1,0:T(8,128)(2,1)} %pad_maximum_fusion.12), channel_id=1, source_target_pairs={{0,8},{4,12},{8,16},{12,20},{16,24},{20,28},{24,0},{28,4},{1,9},{5... | collective-permute-start | bytes 1671176 | tf_op jit(solution)/shard_map/ppermute | solution.py:32
  10.6 20.2 %collective-permute-start.1 = (bf16[128,2176]{1,0:T(8,128)(2,1)}, bf16[128,2176]{1,0:T(8,128)(2,1)}, u32[]{:S(2)}, u32[]{:S(2)}) collective-permute-start(bf16[128,2176]{1,0:T(8,128)(2,1)} %pad_maximum_fusion.12), channel_id=1, source_target_pairs={{0,4},{4,0},{8,12},{12,8},{16,20},{20,16},{24,28},{28,24},{1,5},{5... | collective-permute-start | bytes 1671176 | tf_op jit(solution)/shard_map/ppermute | solution.py:35
  17.8 6.5 %copy-start.12 = (bf16[128,2048]{1,0:T(8,128)(2,1)S(1)}, bf16[128,2048]{1,0:T(8,128)(2,1)}, u32[]{:S(2)}) copy-start(bf16[128,2048]{1,0:T(8,128)(2,1)} %param.7) | copy-start | bytes 1572868
  19.0 26.6 %collective-permute-start.5 = (bf16[128,2048]{1,0:T(8,128)(2,1)}, bf16[128,2048]{1,0:T(8,128)(2,1)S(1)}, u32[]{:S(2)}, u32[]{:S(2)}) collective-permute-start(bf16[128,2048]{1,0:T(8,128)(2,1)} %collective-permute-done.2), channel_id=1, source_target_pairs={{0,8},{4,12},{8,16},{12,20},{16,24},{20,28},{24,0},{28,4},{1,9},{5... | collective-permute-start | bytes 1572872 | tf_op jit(solution)/shard_map/ppermute | solution.py:32
  20.6 25.0 %collective-permute-start.6 = (bf16[128,2048]{1,0:T(8,128)(2,1)}, bf16[128,2048]{1,0:T(8,128)(2,1)S(1)}, u32[]{:S(2)}, u32[]{:S(2)}) collective-permute-start(bf16[128,2048]{1,0:T(8,128)(2,1)} %collective-permute-done.2), channel_id=1, source_target_pairs={{0,4},{4,0},{8,12},{12,8},{16,20},{20,16},{24,28},{28,24},{1,5},{5... | collective-permute-start | bytes 1572872 | tf_op jit(solution)/shard_map/ppermute | solution.py:35
  24.3 9.6 %copy-start.5 = (bf16[128,2048]{1,0:T(8,128)(2,1)S(1)}, bf16[128,2048]{1,0:T(8,128)(2,1)}, u32[]{:S(2)}) copy-start(bf16[128,2048]{1,0:T(8,128)(2,1)} %param.8) | copy-start | bytes 1572868
  30.8 23.0 %collective-permute-start.9 = (bf16[128,2176]{1,0:T(8,128)(2,1)}, bf16[128,2176]{1,0:T(8,128)(2,1)S(1)}, u32[]{:S(2)}, u32[]{:S(2)}) collective-permute-start(bf16[128,2176]{1,0:T(8,128)(2,1)} %collective-permute-done), channel_id=1, source_target_pairs={{0,8},{4,12},{8,16},{12,20},{16,24},{20,28},{24,0},{28,4},{1,9},{5... | collective-permute-start | bytes 1671176 | tf_op jit(solution)/shard_map/ppermute | solution.py:32
  32.4 21.5 %collective-permute-start.10 = (bf16[128,2176]{1,0:T(8,128)(2,1)}, bf16[128,2176]{1,0:T(8,128)(2,1)S(1)}, u32[]{:S(2)}, u32[]{:S(2)}) collective-permute-start(bf16[128,2176]{1,0:T(8,128)(2,1)} %collective-permute-done), channel_id=1, source_target_pairs={{0,4},{4,0},{8,12},{12,8},{16,20},{20,16},{24,28},{28,24},{1,5},{5... | collective-permute-start | bytes 1671176 | tf_op jit(solution)/shard_map/ppermute | solution.py:35
  35.3 59.9 %collective-permute-start.4 = (bf16[128,2176]{1,0:T(8,128)(2,1)}, bf16[128,2176]{1,0:T(8,128)(2,1)S(1)}, u32[]{:S(2)}, u32[]{:S(2)}) collective-permute-start(bf16[128,2176]{1,0:T(8,128)(2,1)} %collective-permute-done.1), channel_id=1, source_target_pairs={{0,24},{4,28},{8,0},{12,4},{16,8},{20,12},{24,16},{28,20},{1,25},{... | collective-permute-start | bytes 1671176 | tf_op jit(solution)/shard_map/ppermute | solution.py:32
  38.9 2.2 %slice-start = ((s8[6291456]{0:T(1024)(128)(4,1)}), s8[4194304]{0:T(1024)(128)(4,1)S(1)}, s32[]{:S(2)}) async-start(s8[6291456]{0:T(1024)(128)(4,1)} %bitcast.60), calls=%async_computation | async-start | bytes 8388608
  39.0 2.9 %slice-start.1 = ((s8[6291456]{0:T(1024)(128)(4,1)}), s8[2097152]{0:T(1024)(128)(4,1)S(1)}, s32[]{:S(2)}) async-start(s8[6291456]{0:T(1024)(128)(4,1)} %bitcast.60), calls=%async_computation.1 | async-start | bytes 4194304
  45.6 31.4 %collective-permute-start.7 = (bf16[128,2048]{1,0:T(8,128)(2,1)S(1)}, bf16[128,2048]{1,0:T(8,128)(2,1)S(1)}, u32[]{:S(2)}, u32[]{:S(2)}) collective-permute-start(bf16[128,2048]{1,0:T(8,128)(2,1)S(1)} %collective-permute-done.5), channel_id=1, source_target_pairs={{0,8},{4,12},{8,16},{12,20},{16,24},{20,28},{24,0},{28,4},{1,9},{5... | collective-permute-start | bytes 1572872 | tf_op jit(solution)/shard_map/ppermute | solution.py:32
  45.6 31.4 %collective-permute-start.8 = (bf16[128,2048]{1,0:T(8,128)(2,1)S(1)}, bf16[128,2048]{1,0:T(8,128)(2,1)S(1)}, u32[]{:S(2)}, u32[]{:S(2)}) collective-permute-start(bf16[128,2048]{1,0:T(8,128)(2,1)S(1)} %collective-permute-done.5), channel_id=1, source_target_pairs={{0,4},{4,0},{8,12},{12,8},{16,20},{20,16},{24,28},{28,24},{1,5},{5... | collective-permute-start | bytes 1572872 | tf_op jit(solution)/shard_map/ppermute | solution.py:35
  54.2 35.0 %collective-permute-start.12 = (bf16[128,2176]{1,0:T(8,128)(2,1)S(1)}, bf16[128,2176]{1,0:T(8,128)(2,1)S(1)}, u32[]{:S(2)}, u32[]{:S(2)}) collective-permute-start(bf16[128,2176]{1,0:T(8,128)(2,1)S(1)} %collective-permute-done.9), channel_id=1, source_target_pairs={{0,8},{4,12},{8,16},{12,20},{16,24},{20,28},{24,0},{28,4},{1,9},{5... | collective-permute-start | bytes 1671176 | tf_op jit(solution)/shard_map/ppermute | solution.py:32
  65.2 24.2 %collective-permute-start.13 = (bf16[128,2176]{1,0:T(8,128)(2,1)S(1)}, bf16[128,2176]{1,0:T(8,128)(2,1)S(1)}, u32[]{:S(2)}, u32[]{:S(2)}) collective-permute-start(bf16[128,2176]{1,0:T(8,128)(2,1)S(1)} %collective-permute-done.9), channel_id=1, source_target_pairs={{0,4},{4,0},{8,12},{12,8},{16,20},{20,16},{24,28},{28,24},{1,5},{5... | collective-permute-start | bytes 1671176 | tf_op jit(solution)/shard_map/ppermute | solution.py:35
  77.0 17.1 %collective-permute-start.11 = (bf16[128,2048]{1,0:T(8,128)(2,1)S(1)}, bf16[128,2048]{1,0:T(8,128)(2,1)S(1)}, u32[]{:S(2)}, u32[]{:S(2)}) collective-permute-start(bf16[128,2048]{1,0:T(8,128)(2,1)S(1)} %collective-permute-done.7), channel_id=1, source_target_pairs={{0,4},{4,0},{8,12},{12,8},{16,20},{20,16},{24,28},{28,24},{1,5},{5... | collective-permute-start | bytes 1572872 | tf_op jit(solution)/shard_map/ppermute | solution.py:35
  78.8 5.5 %copy-start.13 = (bf16[256,768]{1,0:T(8,128)(2,1)S(1)}, bf16[256,768]{1,0:T(8,128)(2,1)}, u32[]{:S(2)}) copy-start(bf16[256,768]{1,0:T(8,128)(2,1)} %get-tuple-element.86) | copy-start | bytes 1179652
  84.3 18.0 %copy-start.4 = (bf16[2048,1536]{1,0:T(8,128)(2,1)}, bf16[2048,1536]{1,0:T(8,128)(2,1)S(1)}, u32[]{:S(2)}) copy-start(bf16[2048,1536]{1,0:T(8,128)(2,1)S(1)} %convolution_convert_fusion) | copy-start | bytes 18874372
  95.2 1.6 copy-start.11
  96.8 1.2 slice-start.4
  96.9 5.4 %copy-start.1 = (bf16[384,1536]{1,0:T(8,128)(2,1)}, bf16[384,1536]{1,0:T(8,128)(2,1)S(1)}, u32[]{:S(2)}) copy-start(bf16[384,1536]{1,0:T(8,128)(2,1)S(1)} %maximum_maximum_fusion) | copy-start | bytes 3538948
  99.9 1.9 copy-start.6
  101.8 2.8 %collective-permute-start.14 = (bf16[2,96,2048]{2,1,0:T(8,128)(2,1)S(1)}, bf16[2,96,2048]{2,1,0:T(8,128)(2,1)}, u32[]{:S(2)}, u32[]{:S(2)}) collective-permute-start(bf16[2,96,2048]{2,1,0:T(8,128)(2,1)S(1)} %get-tuple-element.158), channel_id=1, source_target_pairs={{0,1},{1,0},{2,3},{3,2},{4,5},{5,4},{6,7},{7,6},{8,9},{9,8},{10,11... | collective-permute-start | bytes 2359304 | tf_op jit(solution)/shard_map/ppermute | solution.py:38
  101.8 2.8 %collective-permute-start.15 = (f32[1,128]{1,0:T(1,128)S(1)}, f32[1,128]{1,0:T(1,128)S(1)}, u32[]{:S(2)}, u32[]{:S(2)}) collective-permute-start(f32[1,128]{1,0:T(1,128)S(1)} %add_bitcast_fusion), channel_id=1, source_target_pairs={{0,1},{1,0},{2,3},{3,2},{4,5},{5,4},{6,7},{7,6},{8,9},{9,8},{10,11... | collective-permute-start | bytes 1544 | tf_op jit(solution)/shard_map/ppermute | solution.py:38
  102.3 2.2 %copy-start.8 = (bf16[384,2048]{1,0:T(8,128)(2,1)}, bf16[384,2048]{1,0:T(8,128)(2,1)S(1)}, u32[]{:S(2)}) copy-start(bf16[384,2048]{1,0:T(8,128)(2,1)S(1)} %constant_dynamic-update-slice_fusion.9) | copy-start | bytes 4718596
  104.6 7.3 %collective-permute-start.18 = (bf16[512,1536]{1,0:T(8,128)(2,1)}, bf16[512,1536]{1,0:T(8,128)(2,1)}, u32[]{:S(2)}, u32[]{:S(2)}) collective-permute-start(bf16[512,1536]{1,0:T(8,128)(2,1)} %add_convert_fusion.3), channel_id=1, source_target_pairs={{0,1},{1,0},{2,3},{3,2},{4,5},{5,4},{6,7},{7,6},{8,9},{9,8},{10,11... | collective-permute-start | bytes 4718600 | tf_op jit(solution)/shard_map/ppermute | solution.py:38
  104.7 4.4 %copy-start.2 = (bf16[384,1536]{1,0:T(8,128)(2,1)S(1)}, bf16[384,1536]{1,0:T(8,128)(2,1)}, u32[]{:S(2)}) copy-start(bf16[384,1536]{1,0:T(8,128)(2,1)} %copy-done.1) | copy-start | bytes 3538948
  105.9 16.0 %collective-permute-start.19 = (bf16[128,2048]{1,0:T(8,128)(2,1)S(1)}, bf16[128,2048]{1,0:T(8,128)(2,1)}, u32[]{:S(2)}, u32[]{:S(2)}) collective-permute-start(bf16[128,2048]{1,0:T(8,128)(2,1)S(1)} %slice.137), channel_id=1, source_target_pairs={{0,4},{4,0},{8,12},{12,8},{16,20},{20,16},{24,28},{28,24},{1,5},{5... | collective-permute-start | bytes 1572872 | tf_op jit(solution)/shard_map/ppermute | solution.py:35
  107.4 24.2 %collective-permute-start.20 = (bf16[128,2048]{1,0:T(8,128)(2,1)S(1)}, bf16[128,2048]{1,0:T(8,128)(2,1)}, u32[]{:S(2)}, u32[]{:S(2)}) collective-permute-start(bf16[128,2048]{1,0:T(8,128)(2,1)S(1)} %slice.138), channel_id=1, source_target_pairs={{0,4},{4,0},{8,12},{12,8},{16,20},{20,16},{24,28},{28,24},{1,5},{5... | collective-permute-start | bytes 1572872 | tf_op jit(solution)/shard_map/ppermute | solution.py:35
  109.2 9.5 %slice-start.2 = ((s8[6291456]{0:T(1024)(128)(4,1)}), s8[4194304]{0:T(1024)(128)(4,1)S(1)}, s32[]{:S(2)}) async-start(s8[6291456]{0:T(1024)(128)(4,1)} %bitcast.62), calls=%async_computation.2 | async-start | bytes 8388608
  111.9 6.8 %slice-start.3 = ((s8[6291456]{0:T(1024)(128)(4,1)}), s8[2097152]{0:T(1024)(128)(4,1)S(1)}, s32[]{:S(2)}) async-start(s8[6291456]{0:T(1024)(128)(4,1)} %bitcast.62), calls=%async_computation.3 | async-start | bytes 4194304
  131.6 18.8 %collective-permute-start.22 = (bf16[512,1536]{1,0:T(8,128)(2,1)}, bf16[512,1536]{1,0:T(8,128)(2,1)}, u32[]{:S(2)}, u32[]{:S(2)}) collective-permute-start(bf16[512,1536]{1,0:T(8,128)(2,1)} %fusion.1), channel_id=1, source_target_pairs={{0,1},{1,0},{2,3},{3,2},{4,5},{5,4},{6,7},{7,6},{8,9},{9,8},{10,11... | collective-permute-start | bytes 4718600 | tf_op jit(solution)/shard_map/ppermute | solution.py:38
  131.6 6.5 %copy-start.3 = (bf16[384,1536]{1,0:T(8,128)(2,1)S(1)}, bf16[384,1536]{1,0:T(8,128)(2,1)}, u32[]{:S(2)}) copy-start(bf16[384,1536]{1,0:T(8,128)(2,1)} %copy-done.1) | copy-start | bytes 3538948
  131.6 10.5 %collective-permute-start.23 = (bf16[2,96,2048]{2,1,0:T(8,128)(2,1)}, bf16[2,96,2048]{2,1,0:T(8,128)(2,1)S(1)}, u32[]{:S(2)}, u32[]{:S(2)}) collective-permute-start(bf16[2,96,2048]{2,1,0:T(8,128)(2,1)} %get-tuple-element.157), channel_id=1, source_target_pairs={{0,1},{1,0},{2,3},{3,2},{4,5},{5,4},{6,7},{7,6},{8,9},{9,8},{10,11... | collective-permute-start | bytes 2359304 | tf_op jit(solution)/shard_map/ppermute | solution.py:38
  132.1 54.7 %collective-permute-start.28 = (bf16[512,1536]{1,0:T(8,128)(2,1)}, bf16[512,1536]{1,0:T(8,128)(2,1)S(1)}, u32[]{:S(2)}, u32[]{:S(2)}) collective-permute-start(bf16[512,1536]{1,0:T(8,128)(2,1)} %add_convert_fusion.2), channel_id=1, source_target_pairs={{0,2},{1,3},{2,0},{3,1},{4,6},{5,7},{6,4},{7,5},{8,10},{9,11},{10,... | collective-permute-start | bytes 4718600 | tf_op jit(solution)/shard_map/ppermute | solution.py:38
  133.6 15.0 %collective-permute-start.24 = (bf16[128,2048]{1,0:T(8,128)(2,1)}, bf16[128,2048]{1,0:T(8,128)(2,1)S(1)}, u32[]{:S(2)}, u32[]{:S(2)}) collective-permute-start(bf16[128,2048]{1,0:T(8,128)(2,1)} %convolution_convert_fusion.5), channel_id=1, source_target_pairs={{0,4},{4,0},{8,12},{12,8},{16,20},{20,16},{24,28},{28,24},{1,5},{5... | collective-permute-start | bytes 1572872 | tf_op jit(solution)/shard_map/ppermute | solution.py:35
  135.3 23.4 %collective-permute-start.21 = (bf16[128,2048]{1,0:T(8,128)(2,1)S(1)}, bf16[128,2048]{1,0:T(8,128)(2,1)S(1)}, u32[]{:S(2)}, u32[]{:S(2)}) collective-permute-start(bf16[128,2048]{1,0:T(8,128)(2,1)S(1)} %slice.139), channel_id=1, source_target_pairs={{0,4},{4,0},{8,12},{12,8},{16,20},{20,16},{24,28},{28,24},{1,5},{5... | collective-permute-start | bytes 1572872 | tf_op jit(solution)/shard_map/ppermute | solution.py:35
  138.2 2.7 %copy-start.9 = (bf16[384,2048]{1,0:T(8,128)(2,1)S(1)}, bf16[384,2048]{1,0:T(8,128)(2,1)}, u32[]{:S(2)}) copy-start(bf16[384,2048]{1,0:T(8,128)(2,1)} %convolution_convert_fusion.2) | copy-start | bytes 4718596
  138.2 12.3 %copy-start.7 = (bf16[768,2048]{1,0:T(8,128)(2,1)S(1)}, bf16[768,2048]{1,0:T(8,128)(2,1)}, u32[]{:S(2)}) copy-start(bf16[768,2048]{1,0:T(8,128)(2,1)} %copy-done.6) | copy-start | bytes 9437188
  142.1 10.7 %copy-start.10 = (bf16[256,2048]{1,0:T(8,128)(2,1)S(1)}, bf16[256,2048]{1,0:T(8,128)(2,1)}, u32[]{:S(2)}) copy-start(bf16[256,2048]{1,0:T(8,128)(2,1)} %convolution_convert_fusion.3) | copy-start | bytes 3145732
  142.1 26.4 %collective-permute-start.25 = (bf16[128,2048]{1,0:T(8,128)(2,1)S(1)}, bf16[128,2048]{1,0:T(8,128)(2,1)S(1)}, u32[]{:S(2)}, u32[]{:S(2)}) collective-permute-start(bf16[128,2048]{1,0:T(8,128)(2,1)S(1)} %add_convert_fusion.7), channel_id=1, source_target_pairs={{0,16},{4,20},{8,24},{12,28},{16,0},{20,4},{24,8},{28,12},{1,17},{... | collective-permute-start | bytes 1572872 | tf_op jit(solution)/shard_map/ppermute | solution.py:32
  148.7 33.9 %collective-permute-start.26 = (bf16[128,2048]{1,0:T(8,128)(2,1)S(1)}, bf16[128,2048]{1,0:T(8,128)(2,1)S(1)}, u32[]{:S(2)}, u32[]{:S(2)}) collective-permute-start(bf16[128,2048]{1,0:T(8,128)(2,1)S(1)} %add_convert_fusion.6), channel_id=1, source_target_pairs={{0,24},{4,28},{8,0},{12,4},{16,8},{20,12},{24,16},{28,20},{1,25},{... | collective-permute-start | bytes 1572872 | tf_op jit(solution)/shard_map/ppermute | solution.py:32
  152.2 33.4 %collective-permute-start.16 = (bf16[2,96,2048]{2,1,0:T(8,128)(2,1)S(1)}, bf16[2,96,2048]{2,1,0:T(8,128)(2,1)S(1)}, u32[]{:S(2)}, u32[]{:S(2)}) collective-permute-start(bf16[2,96,2048]{2,1,0:T(8,128)(2,1)S(1)} %get-tuple-element.156), channel_id=1, source_target_pairs={{0,2},{1,3},{2,0},{3,1},{4,6},{5,7},{6,4},{7,5},{8,10},{9,11},{10,... | collective-permute-start | bytes 2359304 | tf_op jit(solution)/shard_map/ppermute | solution.py:38
  158.7 23.9 %collective-permute-start.27 = (bf16[128,2048]{1,0:T(8,128)(2,1)S(1)}, bf16[128,2048]{1,0:T(8,128)(2,1)S(1)}, u32[]{:S(2)}, u32[]{:S(2)}) collective-permute-start(bf16[128,2048]{1,0:T(8,128)(2,1)S(1)} %add_convert_fusion.5), channel_id=1, source_target_pairs={{0,8},{4,12},{8,16},{12,20},{16,24},{20,28},{24,0},{28,4},{1,9},{5... | collective-permute-start | bytes 1572872 | tf_op jit(solution)/shard_map/ppermute | solution.py:32
  168.5 17.1 %collective-permute-start.17 = (f32[1,128]{1,0:T(1,128)S(1)}, f32[1,128]{1,0:T(1,128)S(1)}, u32[]{:S(2)}, u32[]{:S(2)}) collective-permute-start(f32[1,128]{1,0:T(1,128)S(1)} %add.185), channel_id=1, source_target_pairs={{0,2},{1,3},{2,0},{3,1},{4,6},{5,7},{6,4},{7,5},{8,10},{9,11},{10,... | collective-permute-start | bytes 1544 | tf_op jit(solution)/shard_map/ppermute | solution.py:38

commit v3 on v2

v3 whole, which is shorter than its diff:
```python
import jax
import jax.numpy as jnp
from jax import lax
from jax.sharding import PartitionSpec as P

BF = jnp.bfloat16
F32 = jnp.float32
LANES = 128


def dot(a, b, ca, cb):
    return lax.dot_general(a, b, (((ca,), (cb,)), ((), ())), preferred_element_type=F32)


def tie(*values):
    return lax.optimization_barrier(values)


def shards(tokens, out_grad, route_weights, expert_ids, gate_weight, up_weight, down_weight):
    local_experts, width, hidden = gate_weight.shape
    devices = lax.axis_size("expert")
    groups = lax.axis_size("dp")
    num_experts = local_experts * devices
    rows, top_count = expert_ids.shape
    outer = devices // 2
    inner_width = local_experts * hidden
    me = lax.axis_index("expert")
    my_group = lax.axis_index("dp")

    def ring(value, step):
        pairs = [(2 * z + x, 2 * ((z + step) % outer) + x) for z in range(outer) for x in range(2)]
        return lax.ppermute(value, "expert", pairs)

    def cross(value):
        return lax.ppermute(value, "expert", [(i, i ^ 1) for i in range(devices)])

    def swap(value, bit):
        return lax.ppermute(value, "dp", [(i, i ^ bit) for i in range(groups)])

    lanes = jnp.arange(LANES, dtype=jnp.int32)
    dense = jnp.sum(
        jnp.where(
            expert_ids[:, :, None] == lanes, route_weights.astype(F32)[:, :, None], 0.0
        ),
        axis=1,
    ).astype(BF)
    grads = jnp.concatenate([out_grad, dense], axis=1)

    gate_up = jnp.concatenate(
        [gate_weight[e] for e in range(local_experts)] + [up_weight[e] for e in range(local_experts)],
        axis=1,
    )
    down_matrix = down_weight.reshape(inner_width, width)

    def middle(linear, grad_rows):
        cotangent = grad_rows[:, :width]
        routes = grad_rows[:, width:].astype(F32)
        weight = jnp.concatenate(
            [
                jnp.broadcast_to(
                    jnp.sum(
                        jnp.where(lanes == me * local_experts + e, routes, 0.0), axis=1, keepdims=True
                    ),
                    (grad_rows.shape[0], hidden),
                )
                for e in range(local_experts)
            ],
            axis=1,
        )
        gate_linear = linear[:, :inner_width]
        up_linear = linear[:, inner_width:]
        delta_hidden = weight * dot(cotangent, down_matrix, 1, 1)
        logistic = jax.nn.sigmoid(gate_linear)
        activated = gate_linear * logistic
        scaled_hidden = (weight * activated * up_linear).astype(BF)
        delta_gate = delta_hidden * up_linear * logistic * (1.0 + gate_linear * (1.0 - logistic))
        delta_up = delta_hidden * activated
        delta = jnp.concatenate([delta_gate.astype(BF), delta_up.astype(BF)], axis=1)
        return delta, scaled_hidden

    def partial_input(delta):
        return dot(delta, gate_up, 1, 1).astype(BF)

    near = my_group
    chunk_order = [near ^ 3, near ^ 2, near ^ 1, near]
    part = width // groups

    def stacked(blocks, axis=0):
        return jnp.concatenate(blocks, axis=axis) if len(blocks) > 1 else blocks[0]

    def by_chunk(blocks):
        return [
            stacked([lax.dynamic_slice(b, (0, c * part), (b.shape[0], part)) for b in blocks]) for c in chunk_order
        ]

    def cotangents(blocks):
        return stacked([g[:, :width] for g in blocks])

    def add(a, b):
        return (a.astype(F32) + b.astype(F32)).astype(BF)

    flying_a = (ring(tokens, 1), cross(tokens))
    flying_b = (ring(grads, 1), cross(grads))
    gate_up = tie(gate_up, grads)[0]
    token_blocks, grad_blocks, deltas, hiddens, own, other = [], [], [], [], [], []
    first_grad_cross = None
    for step in range(1, outer):
        got = tie(*flying_a, *((deltas[-1], hiddens[-1], own[-1], other[-1], first_grad_cross) if own else ()))
        if own:
            deltas[-1], hiddens[-1], own[-1], other[-1], first_grad_cross = got[2:]
        if step == outer - 1:
            flying_a = (cross(got[0]),)
            flying_back = (ring(first_grad_cross, outer - 1),)
        else:
            flying_a = (ring(got[0], 1), cross(got[0]))
        new_tokens = ((tokens,) if step == 1 else ()) + tuple(got[:2])
        token_blocks.append(new_tokens)
        linear = dot(stacked(new_tokens), gate_up, 1, 0)
        got = tie(*flying_b, linear)
        if step == 1:
            first_grad_cross = got[1]
        flying_b = flying_back if step == outer - 1 else (ring(got[0], 1), cross(got[0]))
        new_grads = ((grads,) if step == 1 else ()) + tuple(got[:2])
        grad_blocks.append(new_grads)
        delta, scaled_hidden = middle(got[2], stacked(new_grads))
        deltas.append(delta)
        hiddens.append(scaled_hidden)
        partial = partial_input(delta)
        if step == 1:
            own.append(partial[:rows])
        own.append(partial[-2 * rows : -rows])
        other.append(partial[-rows:])

    early = [t for blocks in token_blocks[:-1] for t in blocks]
    early_delta = stacked(deltas[:-1])
    early_gate_up = [dot(c, early_delta, 0, 0).astype(BF) for c in by_chunk(early)]
    early_down = dot(stacked(hiddens[:-1]), cotangents([g for b in grad_blocks[:-1] for g in b]), 0, 0).astype(BF)
    late_columns = by_chunk(token_blocks[-1])

    got = tie(*flying_a, early_down, *early_gate_up, *late_columns, *own, *other)
    last_tokens, early_down = got[:2]
    early_gate_up, late_columns = got[2 : 2 + groups], got[2 + groups : 2 + 2 * groups]
    own, other = got[2 + 2 * groups : 2 + 2 * groups + outer], got[2 + 2 * groups + outer :]
    crossed = {s: cross(other[s]) for s in range(1, outer - 1)}
    late_columns = [stacked([a, b]) for a, b in zip(late_columns, by_chunk([last_tokens]))]
    linear = dot(last_tokens, gate_up, 1, 0)
    got = tie(*flying_b, linear, deltas[-1], hiddens[-1], *late_columns)
    last_grads, linear, deltas[-1], hiddens[-1] = got[:4]
    late_columns = got[4:]
    grad_blocks.append((last_grads,))
    load = sum(jnp.sum(g[:, width:].astype(F32), axis=0, keepdims=True) for b in grad_blocks for g in b)
    flying_load = swap(load, 1)
    delta, scaled_hidden = middle(linear, last_grads)
    late_delta = stacked([deltas[-1], delta])
    late_hidden = stacked([hiddens[-1], scaled_hidden])
    late_grads = cotangents([g for b in grad_blocks[-2:] for g in b])

    def gate_up_chunk(index, late_delta, received=None):
        value = dot(late_columns[index], late_delta, 0, 0) + early_gate_up[index].astype(F32)
        return (value if received is None else value + received.astype(F32)).astype(BF)

    def joined(gate_up_part, down_part):
        parts = [gate_up_part[:, i : i + part] for i in range(0, gate_up_part.shape[1], part)]
        down_part = down_part.reshape(-1, width)
        parts += [down_part[:, i : i + part] for i in range(0, width, part)]
        return jnp.concatenate(parts, axis=0)

    def split(message):
        count = 2 * inner_width // part
        wide = jnp.concatenate([message[i * part : (i + 1) * part] for i in range(count)], axis=1)
        rest = message[count * part :]
        size = rest.shape[0] // groups
        narrow = jnp.concatenate([rest[i * size : (i + 1) * size] for i in range(groups)], axis=1)
        return wide, narrow.reshape(local_experts, hidden // groups, width)

    far_other = gate_up_chunk(0, late_delta)
    flying_gate_up = swap(far_other, 1)
    far_other, late_hidden, late_delta = tie(far_other, late_hidden, late_delta)
    all_down = dot(late_hidden, late_grads, 0, 0) + early_down.astype(F32)
    all_down = all_down.astype(BF).reshape(local_experts, groups, hidden // groups, width)
    down = [lax.dynamic_index_in_dim(all_down, c, 1, keepdims=False) for c in chunk_order]
    flying_down = swap(down[0], 1)
    flying_gate_up, flying_load, late_delta, delta, *down = tie(flying_gate_up, flying_load, late_delta, delta, *down)
    far_sum = gate_up_chunk(1, late_delta, flying_gate_up)
    far_sum, flying_down, load, delta, late_delta = tie(far_sum, flying_down, load + flying_load, delta, late_delta)
    flying_load = swap(load, 2)
    message = joined(far_sum, add(down[1], flying_down))
    flying_far = swap(message, 2)
    got = tie(message, delta, late_delta, down[2], other[0], flying_load, crossed[1])
    _, delta, late_delta, near_down, first_other, flying_load, hop = got
    hop = ring(add(own[1], hop), 1)
    last_partial = partial_input(delta)
    crossed[outer - 1] = cross(last_partial)
    near_other = gate_up_chunk(2, late_delta)
    near_gate_up = swap(near_other, 1)
    near_down = swap(near_down, 1)
    near_gate_up, near_down, late_delta = tie(near_gate_up, near_down, late_delta)
    near_gate_up = gate_up_chunk(3, late_delta, near_gate_up)
    near_down = add(down[3], near_down)
    for s in range(2, outer):
        if s == outer - 1:
            hop, crossed[s], near_gate_up, near_down = tie(hop, crossed[s], near_gate_up, near_down)
            crossed[0] = cross(first_other)
        else:
            hop, crossed[s] = tie(hop, crossed[s])
        hop = (own[s].astype(F32) + crossed[s].astype(F32) + hop.astype(F32)).astype(BF)
        hop = ring(hop, 1)
    hop, crossed[0] = tie(hop, crossed[0])
    grad_input = (own[0].astype(F32) + crossed[0].astype(F32) + hop.astype(F32)).astype(BF)

    load = load + flying_load
    expert_load = load[0, :num_experts] * (num_experts / (rows * devices * groups * top_count))
    factor = 1.0 / groups
    flying_far, near_gate_up, near_down, grad_input = tie(flying_far, near_gate_up, near_down, grad_input)
    far_gate_up, far_down = split(flying_far)
    out_gate, out_up = [], []
    for kind, out in ((0, out_gate), (1, out_up)):
        for e in range(local_experts):
            at = slice((kind * local_experts + e) * hidden, (kind * local_experts + e + 1) * hidden)
            value = near_gate_up[:, at].astype(F32) + far_gate_up[:, at].astype(F32)
            out.append((value * factor).astype(BF))
    out_gate, out_up = jnp.stack(out_gate), jnp.stack(out_up)
    out_down = ((near_down.astype(F32) + far_down.astype(F32)) * factor).astype(BF)
    return (grad_input, out_gate, out_up, out_down, expert_load)


def solution(mesh):
    return jax.shard_map(
        shards,
        mesh=mesh,
        in_specs=(
            P(("expert", "dp"), None),
            P(("expert", "dp"), None),
            P(("expert", "dp"), None),
            P(("expert", "dp"), None),
            P("expert", None, None),
            P("expert", None, None),
            P("expert", None, None),
        ),
        out_specs=(
            P(("expert", "dp"), None),
            P("expert", "dp", None),
            P("expert", "dp", None),
            P("expert", "dp", None),
            P(),
        ),
        check_vma=False,
    )
```

time: 193 us -> 170 us (0.88)
  the two profiles are of different devices: /device:TPU:0 before, /device:TPU:16 now
where the time goes in v3:
time: 170 us; the launch traced here: 169 us
  waiting for transfers between devices  64 us (38%)
  matrix products  43.2 us (25%)
  starting transfers between devices  29.2 us (17%)
  local copies, waits for them, and re-layouts  15.5 us (9%)
  other arithmetic  15.4 us (9%)
    dot_general x22, matrix products, dot(): lax.dot_general(a, b, (((ca,), (cb,)), ((), ())), preferred_element_type=...  43.2 us
    ppermute x11, waiting for transfers between devices, cross(): return lax.ppermute(value, 'expert', [(i, i ^ 1) for i in range(devices)])  29.4 us
    ppermute x10, waiting for transfers between devices, ring(): return lax.ppermute(value, 'expert', pairs)  18 us
    ppermute x7, waiting for transfers between devices, swap(): return lax.ppermute(value, 'dp', [(i, i ^ bit) for i in range(groups)])  16.7 us
    ppermute x10, starting transfers between devices, ring(): return lax.ppermute(value, 'expert', pairs)  14.3 us
    ppermute x11, starting transfers between devices, cross(): return lax.ppermute(value, 'expert', [(i, i ^ 1) for i in range(devices)])  11.1 us
    unnamed x34, local copies, waits for them, and re-layouts  7.99 us
    ppermute x7, starting transfers between devices, swap(): return lax.ppermute(value, 'dp', [(i, i ^ bit) for i in range(groups)])  3.91 us
  transfers between devices with their start and end apart: 28, of which 15 were waited for; matrix products, arithmetic and copies ran while one was open for 40% of the time, Pallas kernels for 0%

profile of v3, /device:TPU:16, one launch (start us, length us, event | category | flops | bytes accessed | tf_op | source)
XLA Modules:
  0.0 168.9 jit_solution(1390529556705456247)
XLA Ops:
  0.6 1.6 collective-permute-start.1
  2.2 1.6 collective-permute-start
  5.7 1.9 %pad_maximum_fusion.19 = bf16[128,2176]{1,0:T(8,128)(2,1)} fusion(bf16[128,128]{1,0:T(8,128)(2,1)S(1)} %select_reduce_fusion, bf16[128,2048]{1,0:T(8,128)(2,1)} %param.8), kind=kLoop, calls=%fused_computation.108 | loop fusion | flops 1114112 | bytes 1114112 | tf_op jit(solution)/shard_map/concatenate | solution.py:47
  8.4 3.5 %slice_bitcast_fusion.1 = (bf16[2048,384]{1,0:T(8,128)(2,1)S(1)}, bf16[2048,384]{1,0:T(8,128)(2,1)S(1)}, bf16[2048,384]{1,0:T(8,128)(2,1)S(1)}, bf16[2048,384]{1,0:T(8,128)(2,1)S(1)}) fusion(bf16[2,2048,384]{2,1,0:T(8,128)(2,1)} %param.12, bf16[2,2048,384]{2,1,0:T(8,128)(2,1)} %param.11), kind=kLoop, calls=%fused_computation.44 | loop fusion | bytes 12582912 | tf_op jit(solution)/shard_map/squeeze | solution.py:50
  11.9 3.2 %pad_maximum_fusion = bf16[2048,1536]{1,0:T(8,128)(2,1)} fusion(bf16[2048,384]{1,0:T(8,128)(2,1)S(1)} %get-tuple-element.197, bf16[2048,384]{1,0:T(8,128)(2,1)S(1)} %get-tuple-element.196, bf16[2048,384]{1,0:T(8,128)(2,1)S(1)} %get-tuple-element.258, bf16[2048,384]{1,0:T(8,128)(2,1)S(1)} %get-tuple-element.259), kind=kLoop, calls=%fused_computation | loop fusion | flops 25165824 | bytes 12582912 | tf_op jit(solution)/shard_map/concatenate | solution.py:49
  15.1 1.2 dynamic-slice_dynamic-update-slice_fusion.4
  16.3 1.1 constant_dynamic-update-slice_fusion.2
  17.4 1.5 collective-permute-start.3
  18.9 1.6 collective-permute-start.2
  20.5 1.1 dynamic-slice_dynamic-update-slice_fusion.3
  21.6 1.1 dynamic-slice_dynamic-update-slice_fusion.2
  22.8 5.0 %fusion.8 = f32[384,1536]{1,0:T(8,128)S(1)} fusion(bf16[2048,1536]{1,0:T(8,128)(2,1)} %pad_maximum_fusion, bf16[128,2048]{1,0:T(8,128)(2,1)} %collective-permute-done.1, bf16[128,2048]{1,0:T(8,128)(2,1)} %collective-permute-done, bf16[128,2048]{1,0:T(8,128)(2,1)S(1)} %copy-done.5), kind=kOutput, calls=%fused_computation.26 | convolution fusion | flops 2420637696 | bytes 10223616 | tf_op jit(solution)/shard_map/dot_general | solution.py:12
  27.8 1.5 collective-permute-done.4
  30.7 1.6 collective-permute-start.8
  32.3 1.1 slice_dynamic-update-slice_fusion.6
  34.2 1.1 slice_dynamic-update-slice_fusion.5
  35.3 0.9 fusion.58
  36.5 3.3 %multiply_convert_fusion.1 = (bf16[384,768]{1,0:T(8,128)(2,1)S(1)}, bf16[384,768]{1,0:T(8,128)(2,1)S(1)}, bf16[384,768]{1,0:T(8,128)(2,1)S(1)}) fusion(f32[384,1536]{1,0:T(8,128)S(1)} %fusion.8, f32[384,384]{1,0:T(8,128)S(1)} %broadcast_in_dim.117, f32[384,384]{1,0:T(8,128)S(1)} %broadcast_in_dim.115, bf16[768,2048]{1,0:T(8,128)(2,1)S(1)} %bitcast.64, ...), kind=kOutput, calls=%fused_computation.58 | convolution fusion | flops 1219559424 | bytes 10125312 | tf_op jit(solution)/shard_map/dot_general | solution.py:12
  39.8 2.6 %convolution_convert_fusion.5 = bf16[384,2048]{1,0:T(8,128)(2,1)S(1)} fusion(bf16[2048,1536]{1,0:T(8,128)(2,1)S(1)} %bitcast.69, bf16[384,768]{1,0:T(8,128)(2,1)S(1)} %get-tuple-element.189, bf16[384,768]{1,0:T(8,128)(2,1)S(1)} %get-tuple-element.188), kind=kOutput, calls=%fused_computation.17 | convolution fusion | flops 2419064832 | bytes 9043968 | tf_op jit(solution)/shard_map/dot_general | solution.py:12
  42.7 1.5 collective-permute-start.7
  44.3 2.0 %collective-permute-start.6 = (bf16[128,2048]{1,0:T(8,128)(2,1)S(1)}, bf16[128,2048]{1,0:T(8,128)(2,1)S(1)}, u32[]{:S(2)}, u32[]{:S(2)}) collective-permute-start(bf16[128,2048]{1,0:T(8,128)(2,1)S(1)} %collective-permute-done.2), channel_id=1, source_target_pairs={{0,8},{4,12},{8,16},{12,20},{16,24},{20,28},{24,0},{28,4},{1,9},{5... | collective-permute-start | bytes 1572872 | tf_op jit(solution)/shard_map/ppermute | solution.py:32
  46.5 1.8 %fusion.31 = f32[256,1536]{1,0:T(8,128)S(1)} fusion(bf16[2048,1536]{1,0:T(8,128)(2,1)S(1)} %bitcast.69, bf16[128,2048]{1,0:T(8,128)(2,1)S(1)} %collective-permute-done.3, bf16[128,2048]{1,0:T(8,128)(2,1)S(1)} %collective-permute-done.2), kind=kOutput, calls=%fused_computation.63 | convolution fusion | flops 1612709888 | bytes 8912896 | tf_op jit(solution)/shard_map/dot_general | solution.py:12
  48.3 2.6 %collective-permute-done.9 = bf16[128,2176]{1,0:T(8,128)(2,1)S(1)} collective-permute-done((bf16[128,2176]{1,0:T(8,128)(2,1)}, bf16[128,2176]{1,0:T(8,128)(2,1)S(1)}, u32[]{:S(2)}, u32[]{:S(2)}) %collective-permute-start.9) | collective-permute-done | bytes 557088 | tf_op jit(solution)/shard_map/ppermute | solution.py:35
  50.8 1.5 collective-permute-done.8
  53.0 1.6 collective-permute-start.12
  55.2 1.4 multiply_convert_fusion.9
  56.6 1.8 %convolution_convert_fusion.7 = bf16[256,2048]{1,0:T(8,128)(2,1)S(1)} fusion(bf16[2048,1536]{1,0:T(8,128)(2,1)S(1)} %bitcast.69, bf16[256,768]{1,0:T(8,128)(2,1)S(1)} %get-tuple-element.208, bf16[256,768]{1,0:T(8,128)(2,1)S(1)} %get-tuple-element.207), kind=kOutput, calls=%fused_computation.19 | convolution fusion | flops 1612709888 | bytes 8126464 | tf_op jit(solution)/shard_map/dot_general | solution.py:12
  58.6 3.5 %collective-permute-done.7 = bf16[128,2048]{1,0:T(8,128)(2,1)S(1)} collective-permute-done((bf16[128,2048]{1,0:T(8,128)(2,1)S(1)}, bf16[128,2048]{1,0:T(8,128)(2,1)S(1)}, u32[]{:S(2)}, u32[]{:S(2)}) %collective-permute-start.7) | collective-permute-done | bytes 524320 | tf_op jit(solution)/shard_map/ppermute | solution.py:35
  62.1 1.5 collective-permute-done.6
  64.8 1.4 convolution_convert_fusion.1
  66.3 1.4 convolution_convert_fusion.2
  67.7 1.4 convolution_convert_fusion.3
  69.1 1.4 convolution_convert_fusion.4
  70.6 4.0 %convolution_convert_fusion = bf16[768,2048]{1,0:T(8,128)(2,1)} fusion(bf16[640,2048]{1,0:T(8,128)(2,1)S(1)} %slice_dynamic-update-slice_fusion.3, bf16[256,768]{1,0:T(8,128)(2,1)S(1)} %get-tuple-element.106, bf16[384,768]{1,0:T(8,128)(2,1)S(1)} %get-tuple-element.105), kind=kOutput, calls=%fused_computation.2 | convolution fusion | flops 2016804864 | bytes 6750208 | tf_op jit(solution)/shard_map/dot_general | solution.py:12
  74.7 1.8 %fusion.35 = f32[256,1536]{1,0:T(8,128)S(1)} fusion(bf16[2048,1536]{1,0:T(8,128)(2,1)S(1)} %bitcast.69, bf16[128,2048]{1,0:T(8,128)(2,1)S(1)} %collective-permute-done.7, bf16[128,2048]{1,0:T(8,128)(2,1)S(1)} %collective-permute-done.6), kind=kOutput, calls=%fused_computation.67 | convolution fusion | flops 1612709888 | bytes 8912896 | tf_op jit(solution)/shard_map/dot_general | solution.py:12
  76.5 9.5 %collective-permute-done.12 = bf16[128,2176]{1,0:T(8,128)(2,1)S(1)} collective-permute-done((bf16[128,2176]{1,0:T(8,128)(2,1)S(1)}, bf16[128,2176]{1,0:T(8,128)(2,1)S(1)}, u32[]{:S(2)}, u32[]{:S(2)}) %collective-permute-start.12) | collective-permute-done | bytes 557088 | tf_op jit(solution)/shard_map/ppermute | solution.py:32
  86.5 1.4 multiply_convert_fusion.7
  87.9 1.8 %convolution_convert_fusion.6 = bf16[256,2048]{1,0:T(8,128)(2,1)S(1)} fusion(bf16[2048,1536]{1,0:T(8,128)(2,1)S(1)} %bitcast.69, bf16[256,768]{1,0:T(8,128)(2,1)S(1)} %get-tuple-element.206, bf16[256,768]{1,0:T(8,128)(2,1)S(1)} %get-tuple-element.205), kind=kOutput, calls=%fused_computation.18 | convolution fusion | flops 1612709888 | bytes 8126464 | tf_op jit(solution)/shard_map/dot_general | solution.py:12
  90.7 1.0 fusion.78
  92.1 1.3 multiply_convert_fusion.11
  93.4 1.0 fusion.2
  95.9 3.7 %add_convert_fusion = bf16[768,2048]{1,0:T(8,128)(2,1)S(1)} fusion(bf16[768,2048]{1,0:T(8,128)(2,1)} %convolution_convert_fusion, bf16[384,768]{1,0:T(8,128)(2,1)S(1)} %pad_maximum_fusion.18, bf16[128,2048]{1,0:T(8,128)(2,1)S(1)} %slice-done.4, bf16[128,2048]{1,0:T(8,128)(2,1)S(1)} %slice-done.2, bf16[128,2048]{1,0:T(8,128)(2,1)S(1)} %slice-done.3), kind=kOutput, calls=%fused_computation.1 | convolution fusion | flops 1217396736 | bytes 8454144 | tf_op jit(solution)/shard_map/dot_general | solution.py:12
  100.7 1.8 %collective-permute-done.15 = f32[1,128]{1,0:T(1,128)S(1)} collective-permute-done((f32[1,128]{1,0:T(1,128)S(1)}, f32[1,128]{1,0:T(1,128)S(1)}, u32[]{:S(2)}, u32[]{:S(2)}) %collective-permute-start.15) | collective-permute-done | bytes 544 | tf_op jit(solution)/shard_map/ppermute | solution.py:38
  102.4 1.2 fusion.3
  103.6 1.6 collective-permute-start.18
  105.8 1.5 collective-permute-done.18
  107.3 1.0 fusion.4
  108.4 1.6 collective-permute-start.21
  110.0 1.9 %collective-permute-start.20 = (bf16[128,2048]{1,0:T(8,128)(2,1)S(1)}, bf16[128,2048]{1,0:T(8,128)(2,1)S(1)}, u32[]{:S(2)}, u32[]{:S(2)}) collective-permute-start(bf16[128,2048]{1,0:T(8,128)(2,1)S(1)} %add_convert_fusion.6), channel_id=1, source_target_pairs={{0,8},{4,12},{8,16},{12,20},{16,24},{20,28},{24,0},{28,4},{1,9},{5... | collective-permute-start | bytes 1572872 | tf_op jit(solution)/shard_map/ppermute | solution.py:32
  111.9 1.5 collective-permute-start.17
  113.5 2.1 %convolution_convert_fusion.8 = bf16[128,2048]{1,0:T(8,128)(2,1)S(1)} fusion(bf16[128,1536]{1,0:T(8,128)(2,1)S(1)} %pad_maximum_fusion.27, bf16[2048,1536]{1,0:T(8,128)(2,1)S(1)} %bitcast.69), kind=kOutput, calls=%fused_computation.20 | convolution fusion | flops 805568512 | bytes 7208960 | tf_op jit(solution)/shard_map/dot_general | solution.py:12
  115.6 7.1 %collective-permute-done.21 = bf16[128,2048]{1,0:T(8,128)(2,1)S(1)} collective-permute-done((bf16[128,2048]{1,0:T(8,128)(2,1)S(1)}, bf16[128,2048]{1,0:T(8,128)(2,1)S(1)}, u32[]{:S(2)}, u32[]{:S(2)}) %collective-permute-start.21) | collective-permute-done | bytes 524320 | tf_op jit(solution)/shard_map/ppermute | solution.py:35
  122.7 1.5 collective-permute-start.23
  125.2 1.6 collective-permute-start.22
  126.8 1.2 fusion.5
  128.3 9.3 %collective-permute-done.23 = bf16[128,2048]{1,0:T(8,128)(2,1)S(1)} collective-permute-done((bf16[128,2048]{1,0:T(8,128)(2,1)S(1)}, bf16[128,2048]{1,0:T(8,128)(2,1)S(1)}, u32[]{:S(2)}, u32[]{:S(2)}) %collective-permute-start.23) | collective-permute-done | bytes 524320 | tf_op jit(solution)/shard_map/ppermute | solution.py:35
  138.3 1.6 collective-permute-start.26
  140.5 6.9 %collective-permute-done.27 = bf16[128,2048]{1,0:T(8,128)(2,1)S(1)} collective-permute-done((bf16[128,2048]{1,0:T(8,128)(2,1)S(1)}, bf16[128,2048]{1,0:T(8,128)(2,1)S(1)}, u32[]{:S(2)}, u32[]{:S(2)}) %collective-permute-start.27) | collective-permute-done | bytes 524320 | tf_op jit(solution)/shard_map/ppermute | solution.py:35
  147.4 3.2 %collective-permute-done.26 = bf16[128,2048]{1,0:T(8,128)(2,1)S(1)} collective-permute-done((bf16[128,2048]{1,0:T(8,128)(2,1)S(1)}, bf16[128,2048]{1,0:T(8,128)(2,1)S(1)}, u32[]{:S(2)}, u32[]{:S(2)}) %collective-permute-start.26) | collective-permute-done | bytes 524320 | tf_op jit(solution)/shard_map/ppermute | solution.py:32
  150.6 1.0 add_convert_fusion.3
  151.6 13.3 %collective-permute-done.17 = bf16[2304,512]{1,0:T(8,128)(2,1)S(1)} collective-permute-done((bf16[2304,512]{1,0:T(8,128)(2,1)S(1)}, bf16[2304,512]{1,0:T(8,128)(2,1)S(1)}, u32[]{:S(2)}, u32[]{:S(2)}) %collective-permute-start.17) | collective-permute-done | bytes 2359328 | tf_op jit(solution)/shard_map/ppermute | solution.py:38
  165.2 1.2 fusion.23
  167.0 1.0 pad_maximum_fusion.16
  167.9 1.0 pad_maximum_fusion.15
  (124 shorter events, 16.4 us)
Async XLA Ops:
  0.6 35.6 %copy-start = (bf16[2,384,2048]{2,1,0:T(8,128)(2,1)S(1)}, bf16[2,384,2048]{2,1,0:T(8,128)(2,1)}, u32[]{:S(2)}) copy-start(bf16[2,384,2048]{2,1,0:T(8,128)(2,1)} %param.13) | copy-start | bytes 9437188
  0.6 16.8 %collective-permute-start.1 = (bf16[128,2048]{1,0:T(8,128)(2,1)}, bf16[128,2048]{1,0:T(8,128)(2,1)}, u32[]{:S(2)}, u32[]{:S(2)}) collective-permute-start(bf16[128,2048]{1,0:T(8,128)(2,1)} %param.7), channel_id=1, source_target_pairs={{0,4},{4,0},{8,12},{12,8},{16,20},{20,16},{24,28},{28,24},{1,5},{5... | collective-permute-start | bytes 1572872 | tf_op jit(solution)/shard_map/ppermute | solution.py:35
  2.2 15.2 %collective-permute-start = (bf16[128,2048]{1,0:T(8,128)(2,1)}, bf16[128,2048]{1,0:T(8,128)(2,1)}, u32[]{:S(2)}, u32[]{:S(2)}) collective-permute-start(bf16[128,2048]{1,0:T(8,128)(2,1)} %param.7), channel_id=1, source_target_pairs={{0,8},{4,12},{8,16},{12,20},{16,24},{20,28},{24,0},{28,4},{1,9},{5... | collective-permute-start | bytes 1572872 | tf_op jit(solution)/shard_map/ppermute | solution.py:32
  7.6 20.2 %collective-permute-start.5 = (bf16[128,2176]{1,0:T(8,128)(2,1)}, bf16[128,2176]{1,0:T(8,128)(2,1)}, u32[]{:S(2)}, u32[]{:S(2)}) collective-permute-start(bf16[128,2176]{1,0:T(8,128)(2,1)} %pad_maximum_fusion.19), channel_id=1, source_target_pairs={{0,4},{4,0},{8,12},{12,8},{16,20},{20,16},{24,28},{28,24},{1,5},{5... | collective-permute-start | bytes 1671176 | tf_op jit(solution)/shard_map/ppermute | solution.py:35
  8.1 21.2 %collective-permute-start.4 = (bf16[128,2176]{1,0:T(8,128)(2,1)}, bf16[128,2176]{1,0:T(8,128)(2,1)}, u32[]{:S(2)}, u32[]{:S(2)}) collective-permute-start(bf16[128,2176]{1,0:T(8,128)(2,1)} %pad_maximum_fusion.19), channel_id=1, source_target_pairs={{0,8},{4,12},{8,16},{12,20},{16,24},{20,28},{24,0},{28,4},{1,9},{5... | collective-permute-start | bytes 1671176 | tf_op jit(solution)/shard_map/ppermute | solution.py:32
  15.1 7.6 %copy-start.5 = (bf16[128,2048]{1,0:T(8,128)(2,1)S(1)}, bf16[128,2048]{1,0:T(8,128)(2,1)}, u32[]{:S(2)}) copy-start(bf16[128,2048]{1,0:T(8,128)(2,1)} %param.7) | copy-start | bytes 1572868
  17.4 25.2 %collective-permute-start.3 = (bf16[128,2048]{1,0:T(8,128)(2,1)}, bf16[128,2048]{1,0:T(8,128)(2,1)S(1)}, u32[]{:S(2)}, u32[]{:S(2)}) collective-permute-start(bf16[128,2048]{1,0:T(8,128)(2,1)} %collective-permute-done), channel_id=1, source_target_pairs={{0,4},{4,0},{8,12},{12,8},{16,20},{20,16},{24,28},{28,24},{1,5},{5... | collective-permute-start | bytes 1572872 | tf_op jit(solution)/shard_map/ppermute | solution.py:35
  18.9 23.8 %collective-permute-start.2 = (bf16[128,2048]{1,0:T(8,128)(2,1)}, bf16[128,2048]{1,0:T(8,128)(2,1)S(1)}, u32[]{:S(2)}, u32[]{:S(2)}) collective-permute-start(bf16[128,2048]{1,0:T(8,128)(2,1)} %collective-permute-done), channel_id=1, source_target_pairs={{0,8},{4,12},{8,16},{12,20},{16,24},{20,28},{24,0},{28,4},{1,9},{5... | collective-permute-start | bytes 1572872 | tf_op jit(solution)/shard_map/ppermute | solution.py:32
  27.8 7.5 %copy-start.1 = (bf16[128,2048]{1,0:T(8,128)(2,1)S(1)}, bf16[128,2048]{1,0:T(8,128)(2,1)}, u32[]{:S(2)}) copy-start(bf16[128,2048]{1,0:T(8,128)(2,1)} %param.8) | copy-start | bytes 1572868
  30.1 20.7 %collective-permute-start.9 = (bf16[128,2176]{1,0:T(8,128)(2,1)}, bf16[128,2176]{1,0:T(8,128)(2,1)S(1)}, u32[]{:S(2)}, u32[]{:S(2)}) collective-permute-start(bf16[128,2176]{1,0:T(8,128)(2,1)} %collective-permute-done.4), channel_id=1, source_target_pairs={{0,4},{4,0},{8,12},{12,8},{16,20},{20,16},{24,28},{28,24},{1,5},{5... | collective-permute-start | bytes 1671176 | tf_op jit(solution)/shard_map/ppermute | solution.py:35
  30.7 21.7 %collective-permute-start.8 = (bf16[128,2176]{1,0:T(8,128)(2,1)}, bf16[128,2176]{1,0:T(8,128)(2,1)S(1)}, u32[]{:S(2)}, u32[]{:S(2)}) collective-permute-start(bf16[128,2176]{1,0:T(8,128)(2,1)} %collective-permute-done.4), channel_id=1, source_target_pairs={{0,8},{4,12},{8,16},{12,20},{16,24},{20,28},{24,0},{28,4},{1,9},{5... | collective-permute-start | bytes 1671176 | tf_op jit(solution)/shard_map/ppermute | solution.py:32
  36.3 3.4 %slice-start = ((s8[6291456]{0:T(1024)(128)(4,1)}), s8[4194304]{0:T(1024)(128)(4,1)S(1)}, s32[]{:S(2)}) async-start(s8[6291456]{0:T(1024)(128)(4,1)} %bitcast.68), calls=%async_computation | async-start | bytes 8388608
  36.5 3.3 %slice-start.1 = ((s8[6291456]{0:T(1024)(128)(4,1)}), s8[2097152]{0:T(1024)(128)(4,1)S(1)}, s32[]{:S(2)}) async-start(s8[6291456]{0:T(1024)(128)(4,1)} %bitcast.68), calls=%async_computation.1 | async-start | bytes 4194304
  42.7 19.4 %collective-permute-start.7 = (bf16[128,2048]{1,0:T(8,128)(2,1)S(1)}, bf16[128,2048]{1,0:T(8,128)(2,1)S(1)}, u32[]{:S(2)}, u32[]{:S(2)}) collective-permute-start(bf16[128,2048]{1,0:T(8,128)(2,1)S(1)} %collective-permute-done.2), channel_id=1, source_target_pairs={{0,4},{4,0},{8,12},{12,8},{16,20},{20,16},{24,28},{28,24},{1,5},{5... | collective-permute-start | bytes 1572872 | tf_op jit(solution)/shard_map/ppermute | solution.py:35
  44.3 19.4 %collective-permute-start.6 = (bf16[128,2048]{1,0:T(8,128)(2,1)S(1)}, bf16[128,2048]{1,0:T(8,128)(2,1)S(1)}, u32[]{:S(2)}, u32[]{:S(2)}) collective-permute-start(bf16[128,2048]{1,0:T(8,128)(2,1)S(1)} %collective-permute-done.2), channel_id=1, source_target_pairs={{0,8},{4,12},{8,16},{12,20},{16,24},{20,28},{24,0},{28,4},{1,9},{5... | collective-permute-start | bytes 1572872 | tf_op jit(solution)/shard_map/ppermute | solution.py:32
  52.4 24.1 %collective-permute-start.13 = (bf16[128,2176]{1,0:T(8,128)(2,1)S(1)}, bf16[128,2176]{1,0:T(8,128)(2,1)S(1)}, u32[]{:S(2)}, u32[]{:S(2)}) collective-permute-start(bf16[128,2176]{1,0:T(8,128)(2,1)S(1)} %collective-permute-done.8), channel_id=1, source_target_pairs={{0,4},{4,0},{8,12},{12,8},{16,20},{20,16},{24,28},{28,24},{1,5},{5... | collective-permute-start | bytes 1671176 | tf_op jit(solution)/shard_map/ppermute | solution.py:35
  53.0 33.0 %collective-permute-start.12 = (bf16[128,2176]{1,0:T(8,128)(2,1)S(1)}, bf16[128,2176]{1,0:T(8,128)(2,1)S(1)}, u32[]{:S(2)}, u32[]{:S(2)}) collective-permute-start(bf16[128,2176]{1,0:T(8,128)(2,1)S(1)} %collective-permute-done.8), channel_id=1, source_target_pairs={{0,8},{4,12},{8,16},{12,20},{16,24},{20,28},{24,0},{28,4},{1,9},{5... | collective-permute-start | bytes 1671176 | tf_op jit(solution)/shard_map/ppermute | solution.py:32
  63.6 26.3 %collective-permute-start.11 = (bf16[128,2048]{1,0:T(8,128)(2,1)S(1)}, bf16[128,2048]{1,0:T(8,128)(2,1)S(1)}, u32[]{:S(2)}, u32[]{:S(2)}) collective-permute-start(bf16[128,2048]{1,0:T(8,128)(2,1)S(1)} %collective-permute-done.6), channel_id=1, source_target_pairs={{0,4},{4,0},{8,12},{12,8},{16,20},{20,16},{24,28},{28,24},{1,5},{5... | collective-permute-start | bytes 1572872 | tf_op jit(solution)/shard_map/ppermute | solution.py:35
  64.3 27.5 %collective-permute-start.10 = (bf16[128,2176]{1,0:T(8,128)(2,1)}, bf16[128,2176]{1,0:T(8,128)(2,1)S(1)}, u32[]{:S(2)}, u32[]{:S(2)}) collective-permute-start(bf16[128,2176]{1,0:T(8,128)(2,1)} %collective-permute-done.5), channel_id=1, source_target_pairs={{0,24},{4,28},{8,0},{12,4},{16,8},{20,12},{24,16},{28,20},{1,25},{... | collective-permute-start | bytes 1671176 | tf_op jit(solution)/shard_map/ppermute | solution.py:32
  76.5 13.3 %copy-start.2 = (bf16[128,2176]{1,0:T(8,128)(2,1)}, bf16[128,2176]{1,0:T(8,128)(2,1)S(1)}, u32[]{:S(2)}) copy-start(bf16[128,2176]{1,0:T(8,128)(2,1)S(1)} %collective-permute-done.13) | copy-start | bytes 1671172
  86.0 3.8 %copy-start.3 = (bf16[128,2176]{1,0:T(8,128)(2,1)}, bf16[128,2176]{1,0:T(8,128)(2,1)S(1)}, u32[]{:S(2)}) copy-start(bf16[128,2176]{1,0:T(8,128)(2,1)S(1)} %collective-permute-done.12) | copy-start | bytes 1671172
  90.0 15.8 %collective-permute-start.19 = (bf16[128,2048]{1,0:T(8,128)(2,1)S(1)}, bf16[128,2048]{1,0:T(8,128)(2,1)S(1)}, u32[]{:S(2)}, u32[]{:S(2)}) collective-permute-start(bf16[128,2048]{1,0:T(8,128)(2,1)S(1)} %get-tuple-element.147), channel_id=1, source_target_pairs={{0,4},{4,0},{8,12},{12,8},{16,20},{20,16},{24,28},{28,24},{1,5},{5... | collective-permute-start | bytes 1572872 | tf_op jit(solution)/shard_map/ppermute | solution.py:35
  91.8 2.8 %copy-start.4 = (bf16[128,2176]{1,0:T(8,128)(2,1)}, bf16[128,2176]{1,0:T(8,128)(2,1)S(1)}, u32[]{:S(2)}) copy-start(bf16[128,2176]{1,0:T(8,128)(2,1)S(1)} %collective-permute-done.10) | copy-start | bytes 1671172
  94.4 8.0 %collective-permute-start.14 = (bf16[512,1536]{1,0:T(8,128)(2,1)S(1)}, bf16[512,1536]{1,0:T(8,128)(2,1)S(1)}, u32[]{:S(2)}, u32[]{:S(2)}) collective-permute-start(bf16[512,1536]{1,0:T(8,128)(2,1)S(1)} %fusion.2), channel_id=1, source_target_pairs={{0,1},{1,0},{2,3},{3,2},{4,5},{5,4},{6,7},{7,6},{8,9},{9,8},{10,11... | collective-permute-start | bytes 4718600 | tf_op jit(solution)/shard_map/ppermute | solution.py:38
  94.6 1.0 slice-start.2
  94.6 1.2 slice-start.3
  94.6 1.3 slice-start.4
  100.0 3.7 %collective-permute-start.16 = (bf16[2,96,2048]{2,1,0:T(8,128)(2,1)S(1)}, bf16[2,96,2048]{2,1,0:T(8,128)(2,1)S(1)}, u32[]{:S(2)}, u32[]{:S(2)}) collective-permute-start(bf16[2,96,2048]{2,1,0:T(8,128)(2,1)S(1)} %get-tuple-element.193), channel_id=1, source_target_pairs={{0,1},{1,0},{2,3},{3,2},{4,5},{5,4},{6,7},{7,6},{8,9},{9,8},{10,11... | collective-permute-start | bytes 2359304 | tf_op jit(solution)/shard_map/ppermute | solution.py:38
  100.5 1.9 %collective-permute-start.15 = (f32[1,128]{1,0:T(1,128)S(1)}, f32[1,128]{1,0:T(1,128)S(1)}, u32[]{:S(2)}, u32[]{:S(2)}) collective-permute-start(f32[1,128]{1,0:T(1,128)S(1)} %add_bitcast_fusion), channel_id=1, source_target_pairs={{0,1},{1,0},{2,3},{3,2},{4,5},{5,4},{6,7},{7,6},{8,9},{9,8},{10,11... | collective-permute-start | bytes 1544 | tf_op jit(solution)/shard_map/ppermute | solution.py:38
  103.6 3.6 %collective-permute-start.18 = (f32[1,128]{1,0:T(1,128)S(1)}, f32[1,128]{1,0:T(1,128)S(1)}, u32[]{:S(2)}, u32[]{:S(2)}) collective-permute-start(f32[1,128]{1,0:T(1,128)S(1)} %add.264), channel_id=1, source_target_pairs={{0,2},{1,3},{2,0},{3,1},{4,6},{5,7},{6,4},{7,5},{8,10},{9,11},{10,... | collective-permute-start | bytes 1544 | tf_op jit(solution)/shard_map/ppermute | solution.py:38
  108.3 18.5 %collective-permute-start.24 = (bf16[512,1536]{1,0:T(8,128)(2,1)S(1)}, bf16[512,1536]{1,0:T(8,128)(2,1)S(1)}, u32[]{:S(2)}, u32[]{:S(2)}) collective-permute-start(bf16[512,1536]{1,0:T(8,128)(2,1)S(1)} %fusion.4), channel_id=1, source_target_pairs={{0,1},{1,0},{2,3},{3,2},{4,5},{5,4},{6,7},{7,6},{8,9},{9,8},{10,11... | collective-permute-start | bytes 4718600 | tf_op jit(solution)/shard_map/ppermute | solution.py:38
  108.4 14.3 %collective-permute-start.21 = (bf16[128,2048]{1,0:T(8,128)(2,1)S(1)}, bf16[128,2048]{1,0:T(8,128)(2,1)S(1)}, u32[]{:S(2)}, u32[]{:S(2)}) collective-permute-start(bf16[128,2048]{1,0:T(8,128)(2,1)S(1)} %get-tuple-element.149), channel_id=1, source_target_pairs={{0,4},{4,0},{8,12},{12,8},{16,20},{20,16},{24,28},{28,24},{1,5},{5... | collective-permute-start | bytes 1572872 | tf_op jit(solution)/shard_map/ppermute | solution.py:35
  110.0 14.3 %collective-permute-start.20 = (bf16[128,2048]{1,0:T(8,128)(2,1)S(1)}, bf16[128,2048]{1,0:T(8,128)(2,1)S(1)}, u32[]{:S(2)}, u32[]{:S(2)}) collective-permute-start(bf16[128,2048]{1,0:T(8,128)(2,1)S(1)} %add_convert_fusion.6), channel_id=1, source_target_pairs={{0,8},{4,12},{8,16},{12,20},{16,24},{20,28},{24,0},{28,4},{1,9},{5... | collective-permute-start | bytes 1572872 | tf_op jit(solution)/shard_map/ppermute | solution.py:32
  111.9 53.0 %collective-permute-start.17 = (bf16[2304,512]{1,0:T(8,128)(2,1)S(1)}, bf16[2304,512]{1,0:T(8,128)(2,1)S(1)}, u32[]{:S(2)}, u32[]{:S(2)}) collective-permute-start(bf16[2304,512]{1,0:T(8,128)(2,1)S(1)} %slice_dynamic-update-slice_fusion.7), channel_id=1, source_target_pairs={{0,2},{1,3},{2,0},{3,1},{4,6},{5,7},{6,4},{7,5},{8,10},{9,11},{10,... | collective-permute-start | bytes 7077896 | tf_op jit(solution)/shard_map/ppermute | solution.py:38
  113.5 11.7 %collective-permute-start.25 = (bf16[2,96,2048]{2,1,0:T(8,128)(2,1)S(1)}, bf16[2,96,2048]{2,1,0:T(8,128)(2,1)S(1)}, u32[]{:S(2)}, u32[]{:S(2)}) collective-permute-start(bf16[2,96,2048]{2,1,0:T(8,128)(2,1)S(1)} %get-tuple-element.157), channel_id=1, source_target_pairs={{0,1},{1,0},{2,3},{3,2},{4,5},{5,4},{6,7},{7,6},{8,9},{9,8},{10,11... | collective-permute-start | bytes 2359304 | tf_op jit(solution)/shard_map/ppermute | solution.py:38
  122.7 14.8 %collective-permute-start.23 = (bf16[128,2048]{1,0:T(8,128)(2,1)S(1)}, bf16[128,2048]{1,0:T(8,128)(2,1)S(1)}, u32[]{:S(2)}, u32[]{:S(2)}) collective-permute-start(bf16[128,2048]{1,0:T(8,128)(2,1)S(1)} %convolution_convert_fusion.8), channel_id=1, source_target_pairs={{0,4},{4,0},{8,12},{12,8},{16,20},{20,16},{24,28},{28,24},{1,5},{5... | collective-permute-start | bytes 1572872 | tf_op jit(solution)/shard_map/ppermute | solution.py:35
  124.4 23.1 %collective-permute-start.27 = (bf16[128,2048]{1,0:T(8,128)(2,1)S(1)}, bf16[128,2048]{1,0:T(8,128)(2,1)S(1)}, u32[]{:S(2)}, u32[]{:S(2)}) collective-permute-start(bf16[128,2048]{1,0:T(8,128)(2,1)S(1)} %get-tuple-element.169), channel_id=1, source_target_pairs={{0,4},{4,0},{8,12},{12,8},{16,20},{20,16},{24,28},{28,24},{1,5},{5... | collective-permute-start | bytes 1572872 | tf_op jit(solution)/shard_map/ppermute | solution.py:35
  125.2 12.9 %collective-permute-start.22 = (bf16[128,2048]{1,0:T(8,128)(2,1)S(1)}, bf16[128,2048]{1,0:T(8,128)(2,1)S(1)}, u32[]{:S(2)}, u32[]{:S(2)}) collective-permute-start(bf16[128,2048]{1,0:T(8,128)(2,1)S(1)} %add_convert_fusion.5), channel_id=1, source_target_pairs={{0,8},{4,12},{8,16},{12,20},{16,24},{20,28},{24,0},{28,4},{1,9},{5... | collective-permute-start | bytes 1572872 | tf_op jit(solution)/shard_map/ppermute | solution.py:32
  138.3 12.3 %collective-permute-start.26 = (bf16[128,2048]{1,0:T(8,128)(2,1)S(1)}, bf16[128,2048]{1,0:T(8,128)(2,1)S(1)}, u32[]{:S(2)}, u32[]{:S(2)}) collective-permute-start(bf16[128,2048]{1,0:T(8,128)(2,1)S(1)} %add_convert_fusion.4), channel_id=1, source_target_pairs={{0,8},{4,12},{8,16},{12,20},{16,24},{20,28},{24,0},{28,4},{1,9},{5... | collective-permute-start | bytes 1572872 | tf_op jit(solution)/shard_map/ppermute | solution.py:32
